TPU v7x, 256 devices: a whole 4x4x8 slice. The times are simulated.
256 devices in a mesh: gx: 16 (over z_lo, x), gy: 8 (over y, z_hi), gz: 2 (over core).
Axes of the slice: x: 4, y: 4, z: 8 (z_hi: 2, z_lo: 4; z = z_hi * 4 + z_lo), core: 2. Of those that a mesh axis runs over, the one named last changes fastest.
Arguments:
- state_field: float32 [256, 5, 128, 256], P('gx', None, 'gy', 'gz'), may hold values from -6 to 6
- source: float32 [256, 5, 128, 256], P('gx', None, 'gy', 'gz'), may hold values from -6 to 6
- fluid_mask: int32 [256, 128, 256], P('gx', 'gy', 'gz'), may hold values 0 or 1
- cell_kind: int32 [256, 128, 256], P('gx', 'gy', 'gz'), may hold values from 0 to 2
- boundary_side_number: int32 [256, 128, 256], P('gx', 'gy', 'gz'), may hold values from 0 to 11
- center_matrix: float32 [5, 5], replicated, may hold values from -2.5 to 2.5
- flux_jacobian_blocks: float32 [6, 5, 5], replicated, may hold values from -1 to 1
- wall_matrix: float32 [5, 5], replicated, may hold values from -2.5 to 2.5
- diag_inverse: float32 [256, 5, 5, 128, 256], P('gx', None, None, 'gy', 'gz'), may hold values from -0.01 to 0.1
- lower_coupling: float32 [5, 5], replicated, may hold values from -10 to 10
- upper_neighbour_block: float32 [5, 5], replicated, may hold values from -10 to 10
Outputs:
- update: float32 [256, 5, 128, 256], P('gx', None, 'gy', 'gz')
- residual: float32 [256, 5, 128, 256], P('gx', None, 'gy', 'gz')
Inputs may be any that keep to these rules, and one draw needn't show every extreme that they name: `boundary_side_number`: values 0 to 5 name the face of a cell that is a wall (lower x, upper x, lower y, upper y, lower z, upper z); 6 or more: no wall face. `cell_kind`: 0 full cell, 1 cut cell, 2 small cut cell.
All inputs are finite; a program needn't handle non-finite values. No bound on the sum of `fluid_mask` on one device may be relied on, other than what follows from the above.
Results may differ from a plain program's by a relative error of at most 0.00018.
Values sent between devices are 32-bit elements; how exact they have to be, the bound alone decides.
A program may use at most 64 MiB of HBM per device.

v0:
```python
import jax
import jax.numpy as jnp
from jax import lax
from jax.sharding import PartitionSpec as P


def shifted(block, axis, distance):
    devices = range(lax.axis_size(axis))
    route = [(i - distance, i) for i in devices if i - distance in devices]
    return lax.ppermute(block, axis, route)


def with_halo(block, sides, width):
    for axis, dim in sides:
        count = lax.axis_size(axis)
        forward = [(i, i + 1) for i in range(count - 1)]
        backward = [(target, source) for source, target in forward]
        low = lax.ppermute(
            lax.slice_in_dim(block, block.shape[dim] - width, None, axis=dim), axis, forward
        )
        high = lax.ppermute(lax.slice_in_dim(block, 0, width, axis=dim), axis, backward)
        block = jnp.concatenate([low, block, high], axis=dim)
    return block


def const_apply(matrix, vector):
    return jnp.einsum("ab,...byz->...ayz", matrix, vector, precision=lax.Precision.HIGHEST)


def couple(matrix, transfer):
    return jnp.einsum("ab,bcyz->acyz", matrix, transfer, precision=lax.Precision.HIGHEST)


def volume_operator(blocks, vector):
    return jnp.sum(blocks * vector[..., None, :, :, :], axis=-3)


def cell_product(left, right):
    return jnp.sum(left[:, :, None] * right[None], axis=1)


def flux_residual(
    state_field,
    padded,
    source,
    fluid,
    cell_kind,
    boundary_side_number,
    center_matrix,
    flux_jacobian_blocks,
    wall_matrix,
):
    neighbours = [
        padded[:-2, :, 1:-1, 1:-1],
        padded[2:, :, 1:-1, 1:-1],
        padded[1:-1, :, :-2, 1:-1],
        padded[1:-1, :, 2:, 1:-1],
        padded[1:-1, :, 1:-1, :-2],
        padded[1:-1, :, 1:-1, 2:],
    ]
    walled = const_apply(wall_matrix, state_field)
    flux = const_apply(center_matrix, state_field)
    for facing in range(6):
        at_wall = (boundary_side_number == facing)[:, None]
        flux = flux + jnp.where(
            at_wall, walled, const_apply(flux_jacobian_blocks[facing], neighbours[facing])
        )
    weight = jnp.where(cell_kind == 0, 1.0, jnp.where(cell_kind == 1, 2.0, 4.0)).astype(jnp.float32)
    return fluid[:, None] * (source - flux) * weight[:, None]


def carry_east(transfer, offset):

    def relay_step(turn, carry):
        received, sent = carry
        received = shifted(sent, "gx", 1)
        return (received, volume_operator(transfer, received) + offset)

    received, sent = lax.fori_loop(
        0, lax.axis_size("gx") - 1, relay_step, (jnp.zeros_like(offset), offset)
    )
    return received


def carry_west(transfer, offset):

    def relay_step(turn, carry):
        received, sent = carry
        received = shifted(sent, "gx", -1)
        return (received, volume_operator(transfer, received) + offset)

    received, sent = lax.fori_loop(
        0, lax.axis_size("gx") - 1, relay_step, (jnp.zeros_like(offset), offset)
    )
    return received


def on_device(
    state_field,
    source,
    fluid_mask,
    cell_kind,
    boundary_side_number,
    center_matrix,
    flux_jacobian_blocks,
    wall_matrix,
    diag_inverse,
    lower_coupling,
    upper_neighbour_block,
):
    fluid = fluid_mask.astype(jnp.float32)
    masked = state_field * fluid[:, None]
    padded = with_halo(masked, (("gx", 0), ("gy", 2), ("gz", 3)), 1)
    residual = flux_residual(
        state_field,
        padded,
        source,
        fluid,
        cell_kind,
        boundary_side_number,
        center_matrix,
        flux_jacobian_blocks,
        wall_matrix,
    )
    comps = state_field.shape[1]
    plane_shape = (comps, state_field.shape[2], state_field.shape[3])
    zeroed = jnp.zeros(plane_shape, jnp.float32)
    identity = jnp.broadcast_to(
        jnp.eye(comps, dtype=jnp.float32)[:, :, None, None], (comps, comps) + plane_shape[1:]
    )

    def forward_map(carry, inputs):
        value, transfer = carry
        blocks, term = inputs
        value = volume_operator(blocks, term + const_apply(lower_coupling, value))
        transfer = cell_product(blocks, couple(lower_coupling, transfer))
        return ((value, transfer), None)

    def forward(carry, inputs):
        blocks, term = inputs
        carry = volume_operator(blocks, term + const_apply(lower_coupling, carry))
        return (carry, carry)

    (offset, transfer), unused = lax.scan(forward_map, (zeroed, identity), (diag_inverse, residual))
    incoming = carry_east(transfer, offset)
    final, swept = lax.scan(forward, incoming, (diag_inverse, residual))

    def backward_map(carry, inputs):
        value, transfer = carry
        blocks, term = inputs
        value = term - volume_operator(blocks, const_apply(upper_neighbour_block, value))
        transfer = -cell_product(blocks, couple(upper_neighbour_block, transfer))
        return ((value, transfer), None)

    def backward(carry, inputs):
        blocks, value = inputs
        carry = value - volume_operator(blocks, const_apply(upper_neighbour_block, carry))
        return (carry, carry)

    (offset, transfer), unused = lax.scan(
        backward_map, (zeroed, identity), (diag_inverse, swept), reverse=True
    )
    incoming = carry_west(transfer, offset)
    final, update = lax.scan(backward, incoming, (diag_inverse, swept), reverse=True)
    return (update, residual)


def solution(mesh):
    in_specs = (
        P("gx", None, "gy", "gz"),
        P("gx", None, "gy", "gz"),
        P("gx", "gy", "gz"),
        P("gx", "gy", "gz"),
        P("gx", "gy", "gz"),
        P(),
        P(),
        P(),
        P("gx", None, None, "gy", "gz"),
        P(),
        P(),
    )
    out_specs = (P("gx", None, "gy", "gz"), P("gx", None, "gy", "gz"))
    return jax.shard_map(
        on_device, mesh=mesh, in_specs=in_specs, out_specs=out_specs, check_vma=False
    )
```

profile of v0, /device:TPU:32, one launch (start us, length us, event | category | flops | bytes accessed | tf_op | source)
XLA Modules:
  0.0 459.2 jit_solution(4985408173701451812)
XLA Ops:
  3.2 3.5 collective-permute-start.2
  6.7 4.6 collective-permute-start.3
  13.9 2.2 fusion.31
  16.8 8.2 %collective-permute-start.4 = (f32[18,5,1,128]{3,1,2,0:T(8,128)S(1)}, f32[18,5,1,128]{3,1,2,0:T(8,128)S(1)}, u32[]{:S(2)}, u32[]{:S(2)}) collective-permute-start(f32[18,5,1,128]{3,1,2,0:T(8,128)S(1)} %get-tuple-element.473), channel_id=1, source_target_pairs={{0,2},{2,4},{4,6},{6,8},{8,10},{10,12},{12,14},{1,3},{3,5},{5,7},{... | collective-permute-start | bytes 138248 | tf_op jit(solution)/shard_map/ppermute | solution.py:18
  26.3 2.1 convolution_select_fusion.2
  28.4 6.7 %collective-permute-done.5 = f32[18,5,1,128]{3,1,2,0:T(8,128)S(1)} collective-permute-done((f32[18,5,1,128]{3,1,2,0:T(8,128)S(1)}, f32[18,5,1,128]{3,1,2,0:T(8,128)S(1)}, u32[]{:S(2)}, u32[]{:S(2)}) %collective-permute-start.5) | collective-permute-done | bytes 46112 | tf_op jit(solution)/shard_map/ppermute | solution.py:21
  37.4 2.5 copy.82
  40.0 1.9 collective-permute-start.6
  44.7 3.0 convolution_select_fusion
  47.7 2.2 convolution_select_fusion.1
  49.9 2.8 copy.83
  54.5 2.6 convolution_select_fusion.5
  62.2 28.4 %while.81 = (s32[]{:T(128)}, f32[5,16,128]{2,1,0:T(8,128)S(1)}, f32[5,5,16,128]{3,2,1,0:T(8,128)S(1)}, f32[16,5,5,16,128]{4,3,2,1,0:T(8,128)}, f32[16,5,16,128]{...) while((s32[]{:T(128)}, f32[5,16,128]{2,1,0:T(8,128)S(1)}, f32[5,5,16,128]{3,2,1,0:T(8,128)S(1)}, ...), condition=%wide.region_3.4_spmd, body=%wide.region_0.3_spmd.sunk | while | flops 4249602 | bytes 2130205 | solution.py:144
  91.2 129.6 %while.82 = (s32[]{:T(128)}, f32[5,16,128]{2,1,0:T(8,128)}, f32[5,16,128]{2,1,0:T(8,128)S(1)}, f32[5,5,16,128]{3,2,1,0:T(8,128)S(1)}, f32[5,16,128]{2,1,0:T(8,128)S(1)}, /*index=5*/s32[]{:T(128)}) while((s32[]{:T(128)}, f32[5,16,128]{2,1,0:T(8,128)}, f32[5,16,128]{2,1,0:T(8,128)S(1)}, f32[5,5,16,128]{3,2,1,0:T(8,128)S(1)}, ...), condition=%wide.region_6.7_spmd, body=%wide.region_4.6_spmd.sunk | while | flops 102402 | bytes 737417 | solution.py:79
  91.2 1.9 collective-permute-start
  93.1 6.1 %collective-permute-done = f32[5,16,128]{2,1,0:T(8,128)S(1)} collective-permute-done((f32[5,16,128]{2,1,0:T(8,128)S(1)}, f32[5,16,128]{2,1,0:T(8,128)S(1)}, u32[]{:S(2)}, u32[]{:S(2)}) %collective-permute-start) | collective-permute-done | bytes 40992 | tf_op jit(solution)/shard_map/while/body/eval_jaxpr/ppermute | solution.py:10
  99.8 1.9 collective-permute-start
  101.7 6.1 %collective-permute-done = f32[5,16,128]{2,1,0:T(8,128)S(1)} collective-permute-done((f32[5,16,128]{2,1,0:T(8,128)S(1)}, f32[5,16,128]{2,1,0:T(8,128)S(1)}, u32[]{:S(2)}, u32[]{:S(2)}) %collective-permute-start) | collective-permute-done | bytes 40992 | tf_op jit(solution)/shard_map/while/body/eval_jaxpr/ppermute | solution.py:10
  108.4 1.9 collective-permute-start
  110.4 6.1 %collective-permute-done = f32[5,16,128]{2,1,0:T(8,128)S(1)} collective-permute-done((f32[5,16,128]{2,1,0:T(8,128)S(1)}, f32[5,16,128]{2,1,0:T(8,128)S(1)}, u32[]{:S(2)}, u32[]{:S(2)}) %collective-permute-start) | collective-permute-done | bytes 40992 | tf_op jit(solution)/shard_map/while/body/eval_jaxpr/ppermute | solution.py:10
  117.1 1.9 collective-permute-start
  119.0 6.1 %collective-permute-done = f32[5,16,128]{2,1,0:T(8,128)S(1)} collective-permute-done((f32[5,16,128]{2,1,0:T(8,128)S(1)}, f32[5,16,128]{2,1,0:T(8,128)S(1)}, u32[]{:S(2)}, u32[]{:S(2)}) %collective-permute-start) | collective-permute-done | bytes 40992 | tf_op jit(solution)/shard_map/while/body/eval_jaxpr/ppermute | solution.py:10
  125.7 1.9 collective-permute-start
  127.6 6.1 %collective-permute-done = f32[5,16,128]{2,1,0:T(8,128)S(1)} collective-permute-done((f32[5,16,128]{2,1,0:T(8,128)S(1)}, f32[5,16,128]{2,1,0:T(8,128)S(1)}, u32[]{:S(2)}, u32[]{:S(2)}) %collective-permute-start) | collective-permute-done | bytes 40992 | tf_op jit(solution)/shard_map/while/body/eval_jaxpr/ppermute | solution.py:10
  134.3 1.9 collective-permute-start
  136.2 6.1 %collective-permute-done = f32[5,16,128]{2,1,0:T(8,128)S(1)} collective-permute-done((f32[5,16,128]{2,1,0:T(8,128)S(1)}, f32[5,16,128]{2,1,0:T(8,128)S(1)}, u32[]{:S(2)}, u32[]{:S(2)}) %collective-permute-start) | collective-permute-done | bytes 40992 | tf_op jit(solution)/shard_map/while/body/eval_jaxpr/ppermute | solution.py:10
  142.9 1.9 collective-permute-start
  144.8 6.1 %collective-permute-done = f32[5,16,128]{2,1,0:T(8,128)S(1)} collective-permute-done((f32[5,16,128]{2,1,0:T(8,128)S(1)}, f32[5,16,128]{2,1,0:T(8,128)S(1)}, u32[]{:S(2)}, u32[]{:S(2)}) %collective-permute-start) | collective-permute-done | bytes 40992 | tf_op jit(solution)/shard_map/while/body/eval_jaxpr/ppermute | solution.py:10
  151.5 1.9 collective-permute-start
  153.4 6.5 %collective-permute-done = f32[5,16,128]{2,1,0:T(8,128)S(1)} collective-permute-done((f32[5,16,128]{2,1,0:T(8,128)S(1)}, f32[5,16,128]{2,1,0:T(8,128)S(1)}, u32[]{:S(2)}, u32[]{:S(2)}) %collective-permute-start) | collective-permute-done | bytes 40992 | tf_op jit(solution)/shard_map/while/body/eval_jaxpr/ppermute | solution.py:10
  160.5 1.9 collective-permute-start
  162.4 6.1 %collective-permute-done = f32[5,16,128]{2,1,0:T(8,128)S(1)} collective-permute-done((f32[5,16,128]{2,1,0:T(8,128)S(1)}, f32[5,16,128]{2,1,0:T(8,128)S(1)}, u32[]{:S(2)}, u32[]{:S(2)}) %collective-permute-start) | collective-permute-done | bytes 40992 | tf_op jit(solution)/shard_map/while/body/eval_jaxpr/ppermute | solution.py:10
  169.1 1.9 collective-permute-start
  171.0 6.1 %collective-permute-done = f32[5,16,128]{2,1,0:T(8,128)S(1)} collective-permute-done((f32[5,16,128]{2,1,0:T(8,128)S(1)}, f32[5,16,128]{2,1,0:T(8,128)S(1)}, u32[]{:S(2)}, u32[]{:S(2)}) %collective-permute-start) | collective-permute-done | bytes 40992 | tf_op jit(solution)/shard_map/while/body/eval_jaxpr/ppermute | solution.py:10
  177.7 1.9 collective-permute-start
  179.6 6.1 %collective-permute-done = f32[5,16,128]{2,1,0:T(8,128)S(1)} collective-permute-done((f32[5,16,128]{2,1,0:T(8,128)S(1)}, f32[5,16,128]{2,1,0:T(8,128)S(1)}, u32[]{:S(2)}, u32[]{:S(2)}) %collective-permute-start) | collective-permute-done | bytes 40992 | tf_op jit(solution)/shard_map/while/body/eval_jaxpr/ppermute | solution.py:10
  186.3 1.9 collective-permute-start
  188.3 6.1 %collective-permute-done = f32[5,16,128]{2,1,0:T(8,128)S(1)} collective-permute-done((f32[5,16,128]{2,1,0:T(8,128)S(1)}, f32[5,16,128]{2,1,0:T(8,128)S(1)}, u32[]{:S(2)}, u32[]{:S(2)}) %collective-permute-start) | collective-permute-done | bytes 40992 | tf_op jit(solution)/shard_map/while/body/eval_jaxpr/ppermute | solution.py:10
  194.9 1.9 collective-permute-start
  196.9 6.1 %collective-permute-done = f32[5,16,128]{2,1,0:T(8,128)S(1)} collective-permute-done((f32[5,16,128]{2,1,0:T(8,128)S(1)}, f32[5,16,128]{2,1,0:T(8,128)S(1)}, u32[]{:S(2)}, u32[]{:S(2)}) %collective-permute-start) | collective-permute-done | bytes 40992 | tf_op jit(solution)/shard_map/while/body/eval_jaxpr/ppermute | solution.py:10
  203.6 1.9 collective-permute-start
  205.5 6.1 %collective-permute-done = f32[5,16,128]{2,1,0:T(8,128)S(1)} collective-permute-done((f32[5,16,128]{2,1,0:T(8,128)S(1)}, f32[5,16,128]{2,1,0:T(8,128)S(1)}, u32[]{:S(2)}, u32[]{:S(2)}) %collective-permute-start) | collective-permute-done | bytes 40992 | tf_op jit(solution)/shard_map/while/body/eval_jaxpr/ppermute | solution.py:10
  212.2 1.9 collective-permute-start
  214.1 6.1 %collective-permute-done = f32[5,16,128]{2,1,0:T(8,128)S(1)} collective-permute-done((f32[5,16,128]{2,1,0:T(8,128)S(1)}, f32[5,16,128]{2,1,0:T(8,128)S(1)}, u32[]{:S(2)}, u32[]{:S(2)}) %collective-permute-start) | collective-permute-done | bytes 40992 | tf_op jit(solution)/shard_map/while/body/eval_jaxpr/ppermute | solution.py:10
  220.8 41.1 %while.83 = (s32[]{:T(128)}, f32[5,16,128]{2,1,0:T(8,128)}, f32[16,5,16,128]{3,2,1,0:T(8,128)S(1)}, f32[16,5,5,16,128]{4,3,2,1,0:T(8,128)}, f32[16,5,16,128]{3,1...) while((s32[]{:T(128)}, f32[5,16,128]{2,1,0:T(8,128)}, f32[16,5,16,128]{3,2,1,0:T(8,128)S(1)}, ...), condition=%wide.region_9.10_spmd, body=%wide.region_7.9_spmd.sunk | while | flops 716802 | bytes 737497 | solution.py:146
  262.0 29.2 %while.86 = (s32[]{:T(128)}, f32[5,16,128]{2,1,0:T(8,128)S(1)}, f32[5,5,16,128]{3,2,1,0:T(8,128)S(1)}, f32[16,5,16,128]{3,2,1,0:T(8,128)S(1)}, f32[16,5,5,16,128...) while((s32[]{:T(128)}, f32[5,16,128]{2,1,0:T(8,128)S(1)}, ...), condition=%wide.region_13.14_spmd.clone, body=%wide.region_10.13_spmd.clone.sunk | while | flops 4311044 | bytes 2703683 | solution.py:160
  291.9 124.7 %while.84 = (s32[]{:T(128)}, f32[5,16,128]{2,1,0:T(8,128)}, f32[5,16,128]{2,1,0:T(8,128)S(1)}, f32[5,5,16,128]{3,2,1,0:T(8,128)S(1)}, f32[5,16,128]{2,1,0:T(8,128)S(1)}, /*index=5*/s32[]{:T(128)}) while((s32[]{:T(128)}, f32[5,16,128]{2,1,0:T(8,128)}, f32[5,16,128]{2,1,0:T(8,128)S(1)}, f32[5,5,16,128]{3,2,1,0:T(8,128)S(1)}, ...), condition=%wide.region_16.17_spmd, body=%wide.region_14.16_spmd.sunk | while | flops 102402 | bytes 737417 | solution.py:92
  291.9 1.9 collective-permute-start.1
  293.8 4.0 collective-permute-done.1
  298.4 4.0 collective-permute-start.1
  304.9 6.1 %collective-permute-start.1 = (f32[5,16,128]{2,1,0:T(8,128)S(1)}, f32[5,16,128]{2,1,0:T(8,128)S(1)}, u32[]{:S(2)}, u32[]{:S(2)}) collective-permute-start(f32[5,16,128]{2,1,0:T(8,128)S(1)} %get-tuple-element.798), channel_id=1, source_target_pairs={{16,0},{32,16},{48,32},{64,48},{80,64},{96,80},{112,96},{128,112},... | collective-permute-start | bytes 122888 | tf_op jit(solution)/shard_map/while/body/eval_jaxpr/ppermute | solution.py:10
  313.3 6.3 %collective-permute-start.1 = (f32[5,16,128]{2,1,0:T(8,128)S(1)}, f32[5,16,128]{2,1,0:T(8,128)S(1)}, u32[]{:S(2)}, u32[]{:S(2)}) collective-permute-start(f32[5,16,128]{2,1,0:T(8,128)S(1)} %get-tuple-element.798), channel_id=1, source_target_pairs={{16,0},{32,16},{48,32},{64,48},{80,64},{96,80},{112,96},{128,112},... | collective-permute-start | bytes 122888 | tf_op jit(solution)/shard_map/while/body/eval_jaxpr/ppermute | solution.py:10
  321.9 6.3 %collective-permute-start.1 = (f32[5,16,128]{2,1,0:T(8,128)S(1)}, f32[5,16,128]{2,1,0:T(8,128)S(1)}, u32[]{:S(2)}, u32[]{:S(2)}) collective-permute-start(f32[5,16,128]{2,1,0:T(8,128)S(1)} %get-tuple-element.798), channel_id=1, source_target_pairs={{16,0},{32,16},{48,32},{64,48},{80,64},{96,80},{112,96},{128,112},... | collective-permute-start | bytes 122888 | tf_op jit(solution)/shard_map/while/body/eval_jaxpr/ppermute | solution.py:10
  330.6 6.3 %collective-permute-start.1 = (f32[5,16,128]{2,1,0:T(8,128)S(1)}, f32[5,16,128]{2,1,0:T(8,128)S(1)}, u32[]{:S(2)}, u32[]{:S(2)}) collective-permute-start(f32[5,16,128]{2,1,0:T(8,128)S(1)} %get-tuple-element.798), channel_id=1, source_target_pairs={{16,0},{32,16},{48,32},{64,48},{80,64},{96,80},{112,96},{128,112},... | collective-permute-start | bytes 122888 | tf_op jit(solution)/shard_map/while/body/eval_jaxpr/ppermute | solution.py:10
  339.2 6.3 %collective-permute-start.1 = (f32[5,16,128]{2,1,0:T(8,128)S(1)}, f32[5,16,128]{2,1,0:T(8,128)S(1)}, u32[]{:S(2)}, u32[]{:S(2)}) collective-permute-start(f32[5,16,128]{2,1,0:T(8,128)S(1)} %get-tuple-element.798), channel_id=1, source_target_pairs={{16,0},{32,16},{48,32},{64,48},{80,64},{96,80},{112,96},{128,112},... | collective-permute-start | bytes 122888 | tf_op jit(solution)/shard_map/while/body/eval_jaxpr/ppermute | solution.py:10
  347.8 6.3 %collective-permute-start.1 = (f32[5,16,128]{2,1,0:T(8,128)S(1)}, f32[5,16,128]{2,1,0:T(8,128)S(1)}, u32[]{:S(2)}, u32[]{:S(2)}) collective-permute-start(f32[5,16,128]{2,1,0:T(8,128)S(1)} %get-tuple-element.798), channel_id=1, source_target_pairs={{16,0},{32,16},{48,32},{64,48},{80,64},{96,80},{112,96},{128,112},... | collective-permute-start | bytes 122888 | tf_op jit(solution)/shard_map/while/body/eval_jaxpr/ppermute | solution.py:10
  356.4 6.3 %collective-permute-start.1 = (f32[5,16,128]{2,1,0:T(8,128)S(1)}, f32[5,16,128]{2,1,0:T(8,128)S(1)}, u32[]{:S(2)}, u32[]{:S(2)}) collective-permute-start(f32[5,16,128]{2,1,0:T(8,128)S(1)} %get-tuple-element.798), channel_id=1, source_target_pairs={{16,0},{32,16},{48,32},{64,48},{80,64},{96,80},{112,96},{128,112},... | collective-permute-start | bytes 122888 | tf_op jit(solution)/shard_map/while/body/eval_jaxpr/ppermute | solution.py:10
  365.0 6.3 %collective-permute-start.1 = (f32[5,16,128]{2,1,0:T(8,128)S(1)}, f32[5,16,128]{2,1,0:T(8,128)S(1)}, u32[]{:S(2)}, u32[]{:S(2)}) collective-permute-start(f32[5,16,128]{2,1,0:T(8,128)S(1)} %get-tuple-element.798), channel_id=1, source_target_pairs={{16,0},{32,16},{48,32},{64,48},{80,64},{96,80},{112,96},{128,112},... | collective-permute-start | bytes 122888 | tf_op jit(solution)/shard_map/while/body/eval_jaxpr/ppermute | solution.py:10
  373.6 6.3 %collective-permute-start.1 = (f32[5,16,128]{2,1,0:T(8,128)S(1)}, f32[5,16,128]{2,1,0:T(8,128)S(1)}, u32[]{:S(2)}, u32[]{:S(2)}) collective-permute-start(f32[5,16,128]{2,1,0:T(8,128)S(1)} %get-tuple-element.798), channel_id=1, source_target_pairs={{16,0},{32,16},{48,32},{64,48},{80,64},{96,80},{112,96},{128,112},... | collective-permute-start | bytes 122888 | tf_op jit(solution)/shard_map/while/body/eval_jaxpr/ppermute | solution.py:10
  382.2 6.3 %collective-permute-start.1 = (f32[5,16,128]{2,1,0:T(8,128)S(1)}, f32[5,16,128]{2,1,0:T(8,128)S(1)}, u32[]{:S(2)}, u32[]{:S(2)}) collective-permute-start(f32[5,16,128]{2,1,0:T(8,128)S(1)} %get-tuple-element.798), channel_id=1, source_target_pairs={{16,0},{32,16},{48,32},{64,48},{80,64},{96,80},{112,96},{128,112},... | collective-permute-start | bytes 122888 | tf_op jit(solution)/shard_map/while/body/eval_jaxpr/ppermute | solution.py:10
  390.8 6.3 %collective-permute-start.1 = (f32[5,16,128]{2,1,0:T(8,128)S(1)}, f32[5,16,128]{2,1,0:T(8,128)S(1)}, u32[]{:S(2)}, u32[]{:S(2)}) collective-permute-start(f32[5,16,128]{2,1,0:T(8,128)S(1)} %get-tuple-element.798), channel_id=1, source_target_pairs={{16,0},{32,16},{48,32},{64,48},{80,64},{96,80},{112,96},{128,112},... | collective-permute-start | bytes 122888 | tf_op jit(solution)/shard_map/while/body/eval_jaxpr/ppermute | solution.py:10
  399.4 6.3 %collective-permute-start.1 = (f32[5,16,128]{2,1,0:T(8,128)S(1)}, f32[5,16,128]{2,1,0:T(8,128)S(1)}, u32[]{:S(2)}, u32[]{:S(2)}) collective-permute-start(f32[5,16,128]{2,1,0:T(8,128)S(1)} %get-tuple-element.798), channel_id=1, source_target_pairs={{16,0},{32,16},{48,32},{64,48},{80,64},{96,80},{112,96},{128,112},... | collective-permute-start | bytes 122888 | tf_op jit(solution)/shard_map/while/body/eval_jaxpr/ppermute | solution.py:10
  408.1 6.3 %collective-permute-start.1 = (f32[5,16,128]{2,1,0:T(8,128)S(1)}, f32[5,16,128]{2,1,0:T(8,128)S(1)}, u32[]{:S(2)}, u32[]{:S(2)}) collective-permute-start(f32[5,16,128]{2,1,0:T(8,128)S(1)} %get-tuple-element.798), channel_id=1, source_target_pairs={{16,0},{32,16},{48,32},{64,48},{80,64},{96,80},{112,96},{128,112},... | collective-permute-start | bytes 122888 | tf_op jit(solution)/shard_map/while/body/eval_jaxpr/ppermute | solution.py:10
  416.7 41.6 %while.85 = (s32[]{:T(128)}, f32[5,16,128]{2,1,0:T(8,128)}, f32[16,5,16,128]{3,2,1,0:T(8,128)S(1)}, f32[16,5,16,128]{3,2,1,0:T(8,128)S(1)}, f32[16,5,5,16,128]{4...) while((s32[]{:T(128)}, f32[5,16,128]{2,1,0:T(8,128)}, f32[16,5,16,128]{3,2,1,0:T(8,128)S(1)}, ...), condition=%wide.region_19.20_spmd, body=%wide.region_17.19_spmd.sunk | while | flops 727043 | bytes 696529 | solution.py:164
  (641 shorter events, 199.8 us)
Async XLA Ops:
  0.6 10.6 %copy-start = (f32[5,5]{1,0:T(8,128)S(1)}, f32[5,5]{1,0:T(8,128)}, u32[]{:S(2)}) copy-start(f32[5,5]{1,0:T(8,128)} %param.30) | copy-start | bytes 304
  0.6 10.6 %copy-start.3 = (f32[16,5,16,128]{3,2,1,0:T(8,128)S(1)}, f32[16,5,16,128]{3,2,1,0:T(8,128)}, u32[]{:S(2)}) copy-start(f32[16,5,16,128]{3,2,1,0:T(8,128)} %param.23) | copy-start | bytes 1966084
  1.6 10.9 %copy-start.13 = (f32[16,16,128]{2,1,0:T(8,128)}, f32[16,16,128]{2,1,0:T(8,128)S(1)}, u32[]{:S(2)}) copy-start(f32[16,16,128]{2,1,0:T(8,128)S(1)} %convert_element_type.13) | copy-start | bytes 393220
  3.1 9.4 %copy-start.27 = (s32[16,16,128]{2,1,0:T(8,128)S(1)}, s32[16,16,128]{2,1,0:T(8,128)}, u32[]{:S(2)}) copy-start(s32[16,16,128]{2,1,0:T(8,128)} %param.27) | copy-start | bytes 393220
  3.1 10.2 %copy-start.30 = (f32[6,5,5]{2,0,1:T(8,128)S(1)}, f32[6,5,5]{2,0,1:T(8,128)}, u32[]{:S(2)}) copy-start(f32[6,5,5]{2,0,1:T(8,128)} %param.29) | copy-start | bytes 1804
  3.1 10.8 %copy-start.31 = (f32[5,5]{1,0:T(8,128)S(1)}, f32[5,5]{1,0:T(8,128)}, u32[]{:S(2)}) copy-start(f32[5,5]{1,0:T(8,128)} %param.28) | copy-start | bytes 304
  3.2 13.6 %collective-permute-start.2 = (f32[1,5,16,128]{3,1,2,0:T(8,128)S(1)}, f32[1,5,16,128]{3,1,2,0:T(8,128)S(1)}, u32[]{:S(2)}, u32[]{:S(2)}) collective-permute-start(f32[1,5,16,128]{3,1,2,0:T(8,128)S(1)} %get-tuple-element.475), channel_id=1, source_target_pairs={{0,16},{16,32},{32,48},{48,64},{64,80},{80,96},{96,112},{112,128},... | collective-permute-start | bytes 122888 | tf_op jit(solution)/shard_map/ppermute | solution.py:18
  6.7 10.1 %collective-permute-start.3 = (f32[1,5,16,128]{3,1,2,0:T(8,128)S(1)}, f32[1,5,16,128]{3,1,2,0:T(8,128)S(1)}, u32[]{:S(2)}, u32[]{:S(2)}) collective-permute-start(f32[1,5,16,128]{3,1,2,0:T(8,128)S(1)} %get-tuple-element.476), channel_id=1, source_target_pairs={{16,0},{32,16},{48,32},{64,48},{80,64},{96,80},{112,96},{128,112},... | collective-permute-start | bytes 122888 | tf_op jit(solution)/shard_map/ppermute | solution.py:21
  12.5 3.6 copy-start.28
  16.8 18.4 %copy-start.9 = (f32[1,5,16,128]{3,1,2,0:T(8,128)}, f32[1,5,16,128]{3,1,2,0:T(8,128)S(1)}, u32[]{:S(2)}) copy-start(f32[1,5,16,128]{3,1,2,0:T(8,128)S(1)} %collective-permute-done.3) | copy-start | bytes 122884
  16.8 11.6 %collective-permute-start.4 = (f32[18,5,1,128]{3,1,2,0:T(8,128)S(1)}, f32[18,5,1,128]{3,1,2,0:T(8,128)S(1)}, u32[]{:S(2)}, u32[]{:S(2)}) collective-permute-start(f32[18,5,1,128]{3,1,2,0:T(8,128)S(1)} %get-tuple-element.473), channel_id=1, source_target_pairs={{0,2},{2,4},{4,6},{6,8},{8,10},{10,12},{12,14},{1,3},{3,5},{5,7},{... | collective-permute-start | bytes 138248 | tf_op jit(solution)/shard_map/ppermute | solution.py:18
  25.0 10.2 %collective-permute-start.5 = (f32[18,5,1,128]{3,1,2,0:T(8,128)S(1)}, f32[18,5,1,128]{3,1,2,0:T(8,128)S(1)}, u32[]{:S(2)}, u32[]{:S(2)}) collective-permute-start(f32[18,5,1,128]{3,1,2,0:T(8,128)S(1)} %get-tuple-element.474), channel_id=1, source_target_pairs={{2,0},{4,2},{6,4},{8,6},{10,8},{12,10},{14,12},{3,1},{5,3},{7,5},{... | collective-permute-start | bytes 138248 | tf_op jit(solution)/shard_map/ppermute | solution.py:21
  28.4 6.7 %copy-start.15 = (f32[18,5,1,128]{3,1,2,0:T(8,128)}, f32[18,5,1,128]{3,1,2,0:T(8,128)S(1)}, u32[]{:S(2)}) copy-start(f32[18,5,1,128]{3,1,2,0:T(8,128)S(1)} %collective-permute-done.4) | copy-start | bytes 138244
  40.0 9.9 %collective-permute-start.6 = (f32[18,5,18,1]{2,3,1,0:T(1,128)}, f32[18,5,18,1]{2,3,1,0:T(1,128)}, u32[]{:S(2)}, u32[]{:S(2)}) collective-permute-start(f32[18,5,18,1]{2,3,1,0:T(1,128)} %copy.82), channel_id=1, source_target_pairs={{0,1},{2,3},{4,5},{6,7},{8,9},{10,11},{12,13},{14,15},{16,17},{18,... | collective-permute-start | bytes 19448 | tf_op jit(solution)/shard_map/ppermute | solution.py:18
  43.2 9.6 %collective-permute-start.7 = (f32[18,5,18,1]{2,3,1,0:T(1,128)}, f32[18,5,18,1]{2,3,1,0:T(1,128)}, u32[]{:S(2)}, u32[]{:S(2)}) collective-permute-start(f32[18,5,18,1]{2,3,1,0:T(1,128)} %copy.85), channel_id=1, source_target_pairs={{1,0},{3,2},{5,4},{7,6},{9,8},{11,10},{13,12},{15,14},{17,16},{19,... | collective-permute-start | bytes 19448 | tf_op jit(solution)/shard_map/ppermute | solution.py:21
  44.6 3.1 copy-start.10
  44.6 3.1 copy-start.16
  44.6 3.1 copy-start.26
  49.9 4.6 copy-start.29
  54.5 2.7 copy-start.11
  54.5 2.7 copy-start.17
  54.5 2.7 copy-start.19
  54.5 2.7 copy-start.25
  54.5 4.3 copy-start.12
  57.2 1.6 copy-start.5
  57.2 1.6 copy-start.6
  57.2 1.8 copy-start.7
  57.2 2.1 copy-start.8
  57.2 2.1 copy-start.14
  57.2 2.2 copy-start.23
  57.3 2.1 copy-start.24
  61.1 1.1 copy-start.20
  91.2 8.0 %collective-permute-start = (f32[5,16,128]{2,1,0:T(8,128)S(1)}, f32[5,16,128]{2,1,0:T(8,128)S(1)}, u32[]{:S(2)}, u32[]{:S(2)}) collective-permute-start(f32[5,16,128]{2,1,0:T(8,128)S(1)} %get-tuple-element.732), channel_id=1, source_target_pairs={{0,16},{16,32},{32,48},{48,64},{64,80},{80,96},{96,112},{112,128},... | collective-permute-start | bytes 122888 | tf_op jit(solution)/shard_map/while/body/eval_jaxpr/ppermute | solution.py:10
  99.8 8.0 %collective-permute-start = (f32[5,16,128]{2,1,0:T(8,128)S(1)}, f32[5,16,128]{2,1,0:T(8,128)S(1)}, u32[]{:S(2)}, u32[]{:S(2)}) collective-permute-start(f32[5,16,128]{2,1,0:T(8,128)S(1)} %get-tuple-element.732), channel_id=1, source_target_pairs={{0,16},{16,32},{32,48},{48,64},{64,80},{80,96},{96,112},{112,128},... | collective-permute-start | bytes 122888 | tf_op jit(solution)/shard_map/while/body/eval_jaxpr/ppermute | solution.py:10
  108.4 8.0 %collective-permute-start = (f32[5,16,128]{2,1,0:T(8,128)S(1)}, f32[5,16,128]{2,1,0:T(8,128)S(1)}, u32[]{:S(2)}, u32[]{:S(2)}) collective-permute-start(f32[5,16,128]{2,1,0:T(8,128)S(1)} %get-tuple-element.732), channel_id=1, source_target_pairs={{0,16},{16,32},{32,48},{48,64},{64,80},{80,96},{96,112},{112,128},... | collective-permute-start | bytes 122888 | tf_op jit(solution)/shard_map/while/body/eval_jaxpr/ppermute | solution.py:10
  117.1 8.0 %collective-permute-start = (f32[5,16,128]{2,1,0:T(8,128)S(1)}, f32[5,16,128]{2,1,0:T(8,128)S(1)}, u32[]{:S(2)}, u32[]{:S(2)}) collective-permute-start(f32[5,16,128]{2,1,0:T(8,128)S(1)} %get-tuple-element.732), channel_id=1, source_target_pairs={{0,16},{16,32},{32,48},{48,64},{64,80},{80,96},{96,112},{112,128},... | collective-permute-start | bytes 122888 | tf_op jit(solution)/shard_map/while/body/eval_jaxpr/ppermute | solution.py:10
  125.7 8.0 %collective-permute-start = (f32[5,16,128]{2,1,0:T(8,128)S(1)}, f32[5,16,128]{2,1,0:T(8,128)S(1)}, u32[]{:S(2)}, u32[]{:S(2)}) collective-permute-start(f32[5,16,128]{2,1,0:T(8,128)S(1)} %get-tuple-element.732), channel_id=1, source_target_pairs={{0,16},{16,32},{32,48},{48,64},{64,80},{80,96},{96,112},{112,128},... | collective-permute-start | bytes 122888 | tf_op jit(solution)/shard_map/while/body/eval_jaxpr/ppermute | solution.py:10
  134.3 8.0 %collective-permute-start = (f32[5,16,128]{2,1,0:T(8,128)S(1)}, f32[5,16,128]{2,1,0:T(8,128)S(1)}, u32[]{:S(2)}, u32[]{:S(2)}) collective-permute-start(f32[5,16,128]{2,1,0:T(8,128)S(1)} %get-tuple-element.732), channel_id=1, source_target_pairs={{0,16},{16,32},{32,48},{48,64},{64,80},{80,96},{96,112},{112,128},... | collective-permute-start | bytes 122888 | tf_op jit(solution)/shard_map/while/body/eval_jaxpr/ppermute | solution.py:10
  142.9 8.0 %collective-permute-start = (f32[5,16,128]{2,1,0:T(8,128)S(1)}, f32[5,16,128]{2,1,0:T(8,128)S(1)}, u32[]{:S(2)}, u32[]{:S(2)}) collective-permute-start(f32[5,16,128]{2,1,0:T(8,128)S(1)} %get-tuple-element.732), channel_id=1, source_target_pairs={{0,16},{16,32},{32,48},{48,64},{64,80},{80,96},{96,112},{112,128},... | collective-permute-start | bytes 122888 | tf_op jit(solution)/shard_map/while/body/eval_jaxpr/ppermute | solution.py:10
  151.5 8.4 %collective-permute-start = (f32[5,16,128]{2,1,0:T(8,128)S(1)}, f32[5,16,128]{2,1,0:T(8,128)S(1)}, u32[]{:S(2)}, u32[]{:S(2)}) collective-permute-start(f32[5,16,128]{2,1,0:T(8,128)S(1)} %get-tuple-element.732), channel_id=1, source_target_pairs={{0,16},{16,32},{32,48},{48,64},{64,80},{80,96},{96,112},{112,128},... | collective-permute-start | bytes 122888 | tf_op jit(solution)/shard_map/while/body/eval_jaxpr/ppermute | solution.py:10
  160.5 8.0 %collective-permute-start = (f32[5,16,128]{2,1,0:T(8,128)S(1)}, f32[5,16,128]{2,1,0:T(8,128)S(1)}, u32[]{:S(2)}, u32[]{:S(2)}) collective-permute-start(f32[5,16,128]{2,1,0:T(8,128)S(1)} %get-tuple-element.732), channel_id=1, source_target_pairs={{0,16},{16,32},{32,48},{48,64},{64,80},{80,96},{96,112},{112,128},... | collective-permute-start | bytes 122888 | tf_op jit(solution)/shard_map/while/body/eval_jaxpr/ppermute | solution.py:10
  169.1 8.0 %collective-permute-start = (f32[5,16,128]{2,1,0:T(8,128)S(1)}, f32[5,16,128]{2,1,0:T(8,128)S(1)}, u32[]{:S(2)}, u32[]{:S(2)}) collective-permute-start(f32[5,16,128]{2,1,0:T(8,128)S(1)} %get-tuple-element.732), channel_id=1, source_target_pairs={{0,16},{16,32},{32,48},{48,64},{64,80},{80,96},{96,112},{112,128},... | collective-permute-start | bytes 122888 | tf_op jit(solution)/shard_map/while/body/eval_jaxpr/ppermute | solution.py:10
  177.7 8.0 %collective-permute-start = (f32[5,16,128]{2,1,0:T(8,128)S(1)}, f32[5,16,128]{2,1,0:T(8,128)S(1)}, u32[]{:S(2)}, u32[]{:S(2)}) collective-permute-start(f32[5,16,128]{2,1,0:T(8,128)S(1)} %get-tuple-element.732), channel_id=1, source_target_pairs={{0,16},{16,32},{32,48},{48,64},{64,80},{80,96},{96,112},{112,128},... | collective-permute-start | bytes 122888 | tf_op jit(solution)/shard_map/while/body/eval_jaxpr/ppermute | solution.py:10
  186.3 8.0 %collective-permute-start = (f32[5,16,128]{2,1,0:T(8,128)S(1)}, f32[5,16,128]{2,1,0:T(8,128)S(1)}, u32[]{:S(2)}, u32[]{:S(2)}) collective-permute-start(f32[5,16,128]{2,1,0:T(8,128)S(1)} %get-tuple-element.732), channel_id=1, source_target_pairs={{0,16},{16,32},{32,48},{48,64},{64,80},{80,96},{96,112},{112,128},... | collective-permute-start | bytes 122888 | tf_op jit(solution)/shard_map/while/body/eval_jaxpr/ppermute | solution.py:10
  194.9 8.0 %collective-permute-start = (f32[5,16,128]{2,1,0:T(8,128)S(1)}, f32[5,16,128]{2,1,0:T(8,128)S(1)}, u32[]{:S(2)}, u32[]{:S(2)}) collective-permute-start(f32[5,16,128]{2,1,0:T(8,128)S(1)} %get-tuple-element.732), channel_id=1, source_target_pairs={{0,16},{16,32},{32,48},{48,64},{64,80},{80,96},{96,112},{112,128},... | collective-permute-start | bytes 122888 | tf_op jit(solution)/shard_map/while/body/eval_jaxpr/ppermute | solution.py:10
  203.6 8.0 %collective-permute-start = (f32[5,16,128]{2,1,0:T(8,128)S(1)}, f32[5,16,128]{2,1,0:T(8,128)S(1)}, u32[]{:S(2)}, u32[]{:S(2)}) collective-permute-start(f32[5,16,128]{2,1,0:T(8,128)S(1)} %get-tuple-element.732), channel_id=1, source_target_pairs={{0,16},{16,32},{32,48},{48,64},{64,80},{80,96},{96,112},{112,128},... | collective-permute-start | bytes 122888 | tf_op jit(solution)/shard_map/while/body/eval_jaxpr/ppermute | solution.py:10
  212.2 8.0 %collective-permute-start = (f32[5,16,128]{2,1,0:T(8,128)S(1)}, f32[5,16,128]{2,1,0:T(8,128)S(1)}, u32[]{:S(2)}, u32[]{:S(2)}) collective-permute-start(f32[5,16,128]{2,1,0:T(8,128)S(1)} %get-tuple-element.732), channel_id=1, source_target_pairs={{0,16},{16,32},{32,48},{48,64},{64,80},{80,96},{96,112},{112,128},... | collective-permute-start | bytes 122888 | tf_op jit(solution)/shard_map/while/body/eval_jaxpr/ppermute | solution.py:10
  220.8 41.2 %copy-start.21 = (f32[5,5]{1,0:T(8,128)S(1)}, f32[5,5]{1,0:T(8,128)}, u32[]{:S(2)}) copy-start(f32[5,5]{1,0:T(8,128)} %param.33) | copy-start | bytes 304
  291.9 5.9 %collective-permute-start.1 = (f32[5,16,128]{2,1,0:T(8,128)S(1)}, f32[5,16,128]{2,1,0:T(8,128)S(1)}, u32[]{:S(2)}, u32[]{:S(2)}) collective-permute-start(f32[5,16,128]{2,1,0:T(8,128)S(1)} %get-tuple-element.798), channel_id=1, source_target_pairs={{16,0},{32,16},{48,32},{64,48},{80,64},{96,80},{112,96},{128,112},... | collective-permute-start | bytes 122888 | tf_op jit(solution)/shard_map/while/body/eval_jaxpr/ppermute | solution.py:10
  298.4 5.9 %collective-permute-start.1 = (f32[5,16,128]{2,1,0:T(8,128)S(1)}, f32[5,16,128]{2,1,0:T(8,128)S(1)}, u32[]{:S(2)}, u32[]{:S(2)}) collective-permute-start(f32[5,16,128]{2,1,0:T(8,128)S(1)} %get-tuple-element.798), channel_id=1, source_target_pairs={{16,0},{32,16},{48,32},{64,48},{80,64},{96,80},{112,96},{128,112},... | collective-permute-start | bytes 122888 | tf_op jit(solution)/shard_map/while/body/eval_jaxpr/ppermute | solution.py:10
  304.9 7.8 %collective-permute-start.1 = (f32[5,16,128]{2,1,0:T(8,128)S(1)}, f32[5,16,128]{2,1,0:T(8,128)S(1)}, u32[]{:S(2)}, u32[]{:S(2)}) collective-permute-start(f32[5,16,128]{2,1,0:T(8,128)S(1)} %get-tuple-element.798), channel_id=1, source_target_pairs={{16,0},{32,16},{48,32},{64,48},{80,64},{96,80},{112,96},{128,112},... | collective-permute-start | bytes 122888 | tf_op jit(solution)/shard_map/while/body/eval_jaxpr/ppermute | solution.py:10
  313.3 8.0 %collective-permute-start.1 = (f32[5,16,128]{2,1,0:T(8,128)S(1)}, f32[5,16,128]{2,1,0:T(8,128)S(1)}, u32[]{:S(2)}, u32[]{:S(2)}) collective-permute-start(f32[5,16,128]{2,1,0:T(8,128)S(1)} %get-tuple-element.798), channel_id=1, source_target_pairs={{16,0},{32,16},{48,32},{64,48},{80,64},{96,80},{112,96},{128,112},... | collective-permute-start | bytes 122888 | tf_op jit(solution)/shard_map/while/body/eval_jaxpr/ppermute | solution.py:10
  321.9 8.0 %collective-permute-start.1 = (f32[5,16,128]{2,1,0:T(8,128)S(1)}, f32[5,16,128]{2,1,0:T(8,128)S(1)}, u32[]{:S(2)}, u32[]{:S(2)}) collective-permute-start(f32[5,16,128]{2,1,0:T(8,128)S(1)} %get-tuple-element.798), channel_id=1, source_target_pairs={{16,0},{32,16},{48,32},{64,48},{80,64},{96,80},{112,96},{128,112},... | collective-permute-start | bytes 122888 | tf_op jit(solution)/shard_map/while/body/eval_jaxpr/ppermute | solution.py:10
  330.6 8.0 %collective-permute-start.1 = (f32[5,16,128]{2,1,0:T(8,128)S(1)}, f32[5,16,128]{2,1,0:T(8,128)S(1)}, u32[]{:S(2)}, u32[]{:S(2)}) collective-permute-start(f32[5,16,128]{2,1,0:T(8,128)S(1)} %get-tuple-element.798), channel_id=1, source_target_pairs={{16,0},{32,16},{48,32},{64,48},{80,64},{96,80},{112,96},{128,112},... | collective-permute-start | bytes 122888 | tf_op jit(solution)/shard_map/while/body/eval_jaxpr/ppermute | solution.py:10
  339.2 8.0 %collective-permute-start.1 = (f32[5,16,128]{2,1,0:T(8,128)S(1)}, f32[5,16,128]{2,1,0:T(8,128)S(1)}, u32[]{:S(2)}, u32[]{:S(2)}) collective-permute-start(f32[5,16,128]{2,1,0:T(8,128)S(1)} %get-tuple-element.798), channel_id=1, source_target_pairs={{16,0},{32,16},{48,32},{64,48},{80,64},{96,80},{112,96},{128,112},... | collective-permute-start | bytes 122888 | tf_op jit(solution)/shard_map/while/body/eval_jaxpr/ppermute | solution.py:10
  347.8 8.0 %collective-permute-start.1 = (f32[5,16,128]{2,1,0:T(8,128)S(1)}, f32[5,16,128]{2,1,0:T(8,128)S(1)}, u32[]{:S(2)}, u32[]{:S(2)}) collective-permute-start(f32[5,16,128]{2,1,0:T(8,128)S(1)} %get-tuple-element.798), channel_id=1, source_target_pairs={{16,0},{32,16},{48,32},{64,48},{80,64},{96,80},{112,96},{128,112},... | collective-permute-start | bytes 122888 | tf_op jit(solution)/shard_map/while/body/eval_jaxpr/ppermute | solution.py:10
  356.4 8.0 %collective-permute-start.1 = (f32[5,16,128]{2,1,0:T(8,128)S(1)}, f32[5,16,128]{2,1,0:T(8,128)S(1)}, u32[]{:S(2)}, u32[]{:S(2)}) collective-permute-start(f32[5,16,128]{2,1,0:T(8,128)S(1)} %get-tuple-element.798), channel_id=1, source_target_pairs={{16,0},{32,16},{48,32},{64,48},{80,64},{96,80},{112,96},{128,112},... | collective-permute-start | bytes 122888 | tf_op jit(solution)/shard_map/while/body/eval_jaxpr/ppermute | solution.py:10
  365.0 8.0 %collective-permute-start.1 = (f32[5,16,128]{2,1,0:T(8,128)S(1)}, f32[5,16,128]{2,1,0:T(8,128)S(1)}, u32[]{:S(2)}, u32[]{:S(2)}) collective-permute-start(f32[5,16,128]{2,1,0:T(8,128)S(1)} %get-tuple-element.798), channel_id=1, source_target_pairs={{16,0},{32,16},{48,32},{64,48},{80,64},{96,80},{112,96},{128,112},... | collective-permute-start | bytes 122888 | tf_op jit(solution)/shard_map/while/body/eval_jaxpr/ppermute | solution.py:10
  373.6 8.0 %collective-permute-start.1 = (f32[5,16,128]{2,1,0:T(8,128)S(1)}, f32[5,16,128]{2,1,0:T(8,128)S(1)}, u32[]{:S(2)}, u32[]{:S(2)}) collective-permute-start(f32[5,16,128]{2,1,0:T(8,128)S(1)} %get-tuple-element.798), channel_id=1, source_target_pairs={{16,0},{32,16},{48,32},{64,48},{80,64},{96,80},{112,96},{128,112},... | collective-permute-start | bytes 122888 | tf_op jit(solution)/shard_map/while/body/eval_jaxpr/ppermute | solution.py:10
  382.2 8.0 %collective-permute-start.1 = (f32[5,16,128]{2,1,0:T(8,128)S(1)}, f32[5,16,128]{2,1,0:T(8,128)S(1)}, u32[]{:S(2)}, u32[]{:S(2)}) collective-permute-start(f32[5,16,128]{2,1,0:T(8,128)S(1)} %get-tuple-element.798), channel_id=1, source_target_pairs={{16,0},{32,16},{48,32},{64,48},{80,64},{96,80},{112,96},{128,112},... | collective-permute-start | bytes 122888 | tf_op jit(solution)/shard_map/while/body/eval_jaxpr/ppermute | solution.py:10
  390.8 8.0 %collective-permute-start.1 = (f32[5,16,128]{2,1,0:T(8,128)S(1)}, f32[5,16,128]{2,1,0:T(8,128)S(1)}, u32[]{:S(2)}, u32[]{:S(2)}) collective-permute-start(f32[5,16,128]{2,1,0:T(8,128)S(1)} %get-tuple-element.798), channel_id=1, source_target_pairs={{16,0},{32,16},{48,32},{64,48},{80,64},{96,80},{112,96},{128,112},... | collective-permute-start | bytes 122888 | tf_op jit(solution)/shard_map/while/body/eval_jaxpr/ppermute | solution.py:10
  399.4 8.0 %collective-permute-start.1 = (f32[5,16,128]{2,1,0:T(8,128)S(1)}, f32[5,16,128]{2,1,0:T(8,128)S(1)}, u32[]{:S(2)}, u32[]{:S(2)}) collective-permute-start(f32[5,16,128]{2,1,0:T(8,128)S(1)} %get-tuple-element.798), channel_id=1, source_target_pairs={{16,0},{32,16},{48,32},{64,48},{80,64},{96,80},{112,96},{128,112},... | collective-permute-start | bytes 122888 | tf_op jit(solution)/shard_map/while/body/eval_jaxpr/ppermute | solution.py:10
  408.1 8.0 %collective-permute-start.1 = (f32[5,16,128]{2,1,0:T(8,128)S(1)}, f32[5,16,128]{2,1,0:T(8,128)S(1)}, u32[]{:S(2)}, u32[]{:S(2)}) collective-permute-start(f32[5,16,128]{2,1,0:T(8,128)S(1)} %get-tuple-element.798), channel_id=1, source_target_pairs={{16,0},{32,16},{48,32},{64,48},{80,64},{96,80},{112,96},{128,112},... | collective-permute-start | bytes 122888 | tf_op jit(solution)/shard_map/while/body/eval_jaxpr/ppermute | solution.py:10
  458.3 0.8 copy-start.22
  (47 other events, 29.1 us)
where the time goes:
time: 466 us; the launch traced here: 459 us
  starting transfers between devices  138 us (30%)
  waiting for transfers between devices  126 us (27%)
  other arithmetic  79.7 us (17%)
  matrix products  67.4 us (14%)
  local copies, waits for them, and re-layouts  44.1 us (9%)
    ppermute x30, waiting for transfers between devices, shifted(): return lax.ppermute(block, axis, route)  119 us
    ppermute x30, starting transfers between devices, shifted(): return lax.ppermute(block, axis, route)  117 us
    reduce_sum x94, other arithmetic, volume_operator(): return jnp.sum(blocks * vector[..., None, :, :, :], axis=-3)  61.9 us
    dot_general x72, matrix products, const_apply(): jnp.einsum('ab,...byz->...ayz', matrix, vector, precision=lax.Precision.H...  53.3 us
    while x92, local copies, waits for them, and re-layouts  26.8 us
    dot_general x32, matrix products, couple(): jnp.einsum('ab,bcyz->acyz', matrix, transfer, precision=lax.Precision.HIG...  14.1 us
    ppermute x3, starting transfers between devices, with_halo(): lax.ppermute(lax.slice_in_dim(block, block.shape[dim] - width, None, axis...  13.6 us
    sub x16, other arithmetic, backward(): value - volume_operator(blocks, const_apply(upper_neighbour_block, carry))  10.1 us
  transfers between devices with their start and end apart: 36, of which 31 were waited for; matrix products, arithmetic and copies ran while one was open for 4% of the time, Pallas kernels for 0%

commit v1 on v0

v1 whole, which is shorter than its diff:
```python
import functools

import jax
import jax.numpy as jnp
from jax import lax
from jax.experimental import pallas as pl
from jax.experimental.pallas import tpu as pltpu
from jax.sharding import PartitionSpec as P

MESH = pl.DeviceIdType.MESH
F32 = jnp.float32
ROWS_T = 32
ROWS_B = 56
ROWS_V = 8


def aligned(start, size):
    return pl.ds(pl.multiple_of(start, 8), size)


def total(terms):
    terms = list(terms)
    while len(terms) > 1:
        terms = [a + b for a, b in zip(terms[::2], terms[1::2])] + terms[len(terms) & ~1:]
    return terms[0]


def kernel(
    n, ny,
    state_hbm, source_hbm, fluid_hbm, kind_hbm, side_hbm, diag_hbm,
    center, jac, wall, lower, upper,
    update_hbm, residual_hbm,
    state, source, fluid, kind, side, diag,
    masked, ysend, yrecv, zrecv,
    dl, du, tf, g, sw, res, upd,
    send_t, recv_t, send_b, recv_b, send_v, recv_v, send_r, recv_r,
    in_sem, out_sem, halo_send, halo_recv, x_send, x_recv,
):
    planes, comps, rows, lanes = state.shape
    cells = comps * rows
    me = lax.axis_index("gx")
    my = lax.axis_index("gy")
    mz = lax.axis_index("gz")
    east, west = lax.rem(me + 1, n), lax.rem(me + n - 1, n)
    north, south = lax.rem(my + 1, ny), lax.rem(my + ny - 1, ny)

    loads = [
        pltpu.make_async_copy(hbm, vmem, in_sem.at[i])
        for i, (hbm, vmem) in enumerate(
            [(state_hbm, state), (fluid_hbm, fluid), (diag_hbm, diag), (source_hbm, source), (side_hbm, side), (kind_hbm, kind)]
        )
    ]
    for load in loads:
        load.start()

    barrier = pltpu.get_barrier_semaphore()
    for k in range(1, n):
        pl.semaphore_signal(barrier, inc=1, device_id={"gx": lax.rem(me + k, n)}, device_id_type=MESH)
    for other in (north, south):
        pl.semaphore_signal(barrier, inc=1, device_id={"gy": other}, device_id_type=MESH)
    pl.semaphore_signal(barrier, inc=1, device_id={"gz": 1 - mz}, device_id_type=MESH)

    loads[0].wait()
    loads[1].wait()

    def mask_plane(x, _):
        keep = fluid[x].astype(F32)
        for c in range(comps):
            masked[aligned((x + 1) * cells + c * rows, rows), :] = state[x, c] * keep
        return 0

    lax.fori_loop(0, planes, mask_plane, 0)
    ysend[0] = masked[pl.ds(cells + rows - 1, planes * comps, stride=rows), :]
    ysend[1] = masked[pl.ds(cells, planes * comps, stride=rows), :]
    pl.semaphore_wait(barrier, n + 2)

    def remote(src, dst, send_sem, recv_sem, where):
        return pltpu.make_async_remote_copy(
            src_ref=src, dst_ref=dst, send_sem=send_sem, recv_sem=recv_sem, device_id=where, device_id_type=MESH
        )

    halos = [
        remote(ysend.at[0], yrecv.at[0], halo_send.at[0], halo_recv.at[0], {"gy": north}),
        remote(ysend.at[1], yrecv.at[1], halo_send.at[1], halo_recv.at[1], {"gy": south}),
        remote(
            masked.at[pl.ds(planes * cells, cells)], masked.at[pl.ds(0, cells)],
            halo_send.at[2], halo_recv.at[2], {"gx": east},
        ),
        remote(
            masked.at[pl.ds(cells, cells)], masked.at[pl.ds((planes + 1) * cells, cells)],
            halo_send.at[3], halo_recv.at[3], {"gx": west},
        ),
        remote(masked.at[pl.ds(cells, planes * cells)], zrecv, halo_send.at[4], halo_recv.at[4], {"gz": 1 - mz}),
    ]
    for halo in halos:
        halo.start()

    loads[2].wait()

    def products(x, _):
        for a in range(comps):
            row = [diag[x, a, b] for b in range(comps)]
            for c in range(comps):
                dl[x, a, c] = total(row[b] * lower[b, c] for b in range(comps))
                du[x, a, c] = total(row[b] * upper[b, c] for b in range(comps))
        return 0

    lax.fori_loop(0, planes, products, 0)

    def columns(ref, x, half):
        return [ref[x, :, b, aligned(half * 8, 8), :] for b in range(comps)]

    def times(block, column):
        return total(block[b] * column[b][None] for b in range(comps))

    def exchange(src, dst, size, slot, k):
        peer = lax.rem(me + k, n)
        return remote(
            src.at[aligned(peer * size, size)], dst.at[aligned(me * size, size)],
            x_send.at[slot, k], x_recv.at[slot, k], {"gx": peer},
        )

    def start_all(src, dst, size, slot):
        def one(k, _):
            exchange(src, dst, size, slot, k).start()
            return 0

        lax.fori_loop(1, n, one, 0)
        dst[aligned(me * size, size), :] = src[aligned(me * size, size), :]

    def wait_all(src, dst, size, slot):
        def one(k, _):
            exchange(src, dst, size, slot, k).wait_recv()
            return 0

        lax.fori_loop(1, n, one, 0)

    def wait_sent(src, dst, size, slot):
        def one(k, _):
            exchange(src, dst, size, slot, k).wait_send()
            return 0

        lax.fori_loop(1, n, one, 0)

    def forward_maps(half, _):
        def step(x, held):
            block = columns(dl, x, half)
            held = [times(block, column) for column in held]
            for b in range(comps):
                tf[x, :, b, aligned(half * 8, 8), :] = held[b]
            return held

        first = columns(dl, 0, half)
        for b in range(comps):
            tf[0, :, b, aligned(half * 8, 8), :] = first[b]
        last = lax.fori_loop(1, planes, step, first)
        for a in range(comps):
            for b in range(comps):
                send_t[pl.ds(half * 8 * ROWS_T + a * comps + b, 8, stride=ROWS_T), :] = last[b][a]
        return 0

    for half in range(rows // 8):
        forward_maps(half, 0)
    start_all(send_t, recv_t, ROWS_T, 0)

    def backward_maps(half, _):
        def through(turn, held):
            x = planes - 2 - turn
            block = columns(du, x, half)
            return [tf[x, :, b, aligned(half * 8, 8), :] - times(block, held[b]) for b in range(comps)]

        def back(turn, held):
            x = planes - 2 - turn
            block = columns(du, x, half)
            return [-times(block, column) for column in held]

        last = lax.fori_loop(0, planes - 1, through, columns(tf, planes - 1, half))
        for a in range(comps):
            for b in range(comps):
                send_b[pl.ds(half * 8 * ROWS_B + a * comps + b, 8, stride=ROWS_B), :] = last[b][a]
        last = lax.fori_loop(0, planes - 1, back, [-column for column in columns(du, planes - 1, half)])
        for a in range(comps):
            for b in range(comps):
                send_b[pl.ds(half * 8 * ROWS_B + 25 + a * comps + b, 8, stride=ROWS_B), :] = last[b][a]
        return 0

    for half in range(rows // 8):
        backward_maps(half, 0)
    start_all(send_b, recv_b, ROWS_B, 1)

    for halo in halos:
        halo.wait_recv()
    yrecv[0] = jnp.where(my == 0, 0.0, yrecv[0])
    yrecv[1] = jnp.where(my == ny - 1, 0.0, yrecv[1])
    masked[0:cells, :] = jnp.where(me == 0, 0.0, masked[0:cells, :])
    top = pl.ds((planes + 1) * cells, cells)
    masked[top, :] = jnp.where(me == n - 1, 0.0, masked[top, :])
    for i in range(3, 6):
        loads[i].wait()

    row_id = lax.broadcasted_iota(jnp.int32, (rows, lanes), 0)
    lane_id = lax.broadcasted_iota(jnp.int32, (rows, lanes), 1)
    from_low = jnp.where(mz == 0, 0.0, 1.0).astype(F32)
    from_high = 1.0 - from_low

    def residual_planes(step, _):
        xs = (2 * step, 2 * step + 1)
        sides = [side[x] for x in xs]
        flux = [[None] * comps for _ in xs]

        def add(matrix, b, values):
            for a in range(comps):
                weight = matrix(a, b)
                for i, value in enumerate(values):
                    term = weight * value
                    flux[i][a] = term if flux[i][a] is None else flux[i][a] + term

        for b in range(comps):
            own = [state[x, b] for x in xs]
            add(lambda a, b: center[a, b], b, own)
            add(lambda a, b: wall[a, b], b, [jnp.where(s < 6, v, 0.0) for s, v in zip(sides, own)])
            here = [masked[aligned((x + 1) * cells + b * rows, rows), :] for x in xs]
            other = [zrecv[aligned(x * cells + b * rows, rows), :] for x in xs]
            neighbours = [
                [masked[aligned(x * cells + b * rows, rows), :] for x in xs],
                [masked[aligned((x + 2) * cells + b * rows, rows), :] for x in xs],
                [
                    jnp.where(row_id == 0, yrecv[0, pl.ds(x * comps + b, 1), :], pltpu.roll(v, 1, 0))
                    for x, v in zip(xs, here)
                ],
                [
                    jnp.where(row_id == rows - 1, yrecv[1, pl.ds(x * comps + b, 1), :], pltpu.roll(v, rows - 1, 0))
                    for x, v in zip(xs, here)
                ],
                [pltpu.roll(jnp.where(lane_id == lanes - 1, o * from_low, v), 1, 1) for o, v in zip(other, here)],
                [pltpu.roll(jnp.where(lane_id == 0, o * from_high, v), lanes - 1, 1) for o, v in zip(other, here)],
            ]
            for d in range(6):
                add(
                    lambda a, b: jac[d, a, b], b,
                    [jnp.where(s == d, 0.0, v) for s, v in zip(sides, neighbours[d])],
                )
        for i, x in enumerate(xs):
            flag = kind[x]
            weight = jnp.where(flag == 0, 1.0, jnp.where(flag == 1, 2.0, 4.0)) * fluid[x].astype(F32)
            out = [(source[x, a] - flux[i][a]) * weight for a in range(comps)]
            for a in range(comps):
                res[x, a] = out[a]
            for a in range(comps):
                g[x, a] = total(diag[x, a, b] * out[b] for b in range(comps))
        return 0

    lax.fori_loop(0, planes // 2, residual_planes, 0)
    res_out = pltpu.make_async_copy(res, residual_hbm, out_sem.at[0])
    res_out.start()

    def forward(x, held):
        held = [
            g[x, a] + total(dl[x, a, b] * held[b] for b in range(comps)) for a in range(comps)
        ]
        for a in range(comps):
            sw[x, a] = held[a]
        return held

    def backward(turn, held):
        x = planes - 1 - turn
        return [
            sw[x, a] - total(du[x, a, b] * held[b] for b in range(comps)) for a in range(comps)
        ]

    zeros = [jnp.zeros((rows, lanes), F32)] * comps
    held = lax.fori_loop(0, planes, forward, zeros)
    for c in range(comps):
        send_v[0, pl.ds(c, rows, stride=ROWS_V), :] = held[c]
    start_all(send_v.at[0], recv_v.at[0], ROWS_V, 2)
    held = lax.fori_loop(0, planes, backward, zeros)
    for c in range(comps):
        send_v[1, pl.ds(c, rows, stride=ROWS_V), :] = held[c]
    start_all(send_v.at[1], recv_v.at[1], ROWS_V, 3)

    def apply(ref, start, vector):
        return total(ref[pl.ds(start + b, comps, stride=comps), :] * vector[b:b + 1] for b in range(comps))

    wait_all(send_t, recv_t, ROWS_T, 0)
    wait_all(send_v.at[0], recv_v.at[0], ROWS_V, 2)
    came = jnp.zeros((comps, lanes), F32)
    forward_in = []
    for i in range(n):
        forward_in.append(came)
        send_r[0, pl.ds(i * ROWS_V, comps), :] = came
        if i < n - 1:
            came = recv_v[0, pl.ds(i * ROWS_V, comps), :] + apply(recv_t, i * ROWS_T, came)
    start_all(send_r.at[0], recv_r.at[0], ROWS_V, 4)
    wait_all(send_b, recv_b, ROWS_B, 1)
    wait_all(send_v.at[1], recv_v.at[1], ROWS_V, 3)
    came = jnp.zeros((comps, lanes), F32)
    for i in range(n - 1, -1, -1):
        send_r[1, pl.ds(i * ROWS_V, comps), :] = came
        if i > 0:
            came = (
                recv_v[1, pl.ds(i * ROWS_V, comps), :] + apply(recv_b, i * ROWS_B, forward_in[i])
                + apply(recv_b, i * ROWS_B + 25, came)
            )
    start_all(send_r.at[1], recv_r.at[1], ROWS_V, 5)

    wait_all(send_r.at[0], recv_r.at[0], ROWS_V, 4)
    held = [recv_r[0, pl.ds(c, rows, stride=ROWS_V), :] for c in range(comps)]
    lax.fori_loop(0, planes, forward, held)
    wait_all(send_r.at[1], recv_r.at[1], ROWS_V, 5)
    held = [recv_r[1, pl.ds(c, rows, stride=ROWS_V), :] for c in range(comps)]

    def finish(turn, held):
        x = planes - 1 - turn
        held = backward(turn, held)
        for a in range(comps):
            upd[x, a] = held[a]
        return held

    lax.fori_loop(0, planes, finish, held)
    upd_out = pltpu.make_async_copy(upd, update_hbm, out_sem.at[1])
    upd_out.start()
    for halo in halos:
        halo.wait_send()
    wait_sent(send_t, recv_t, ROWS_T, 0)
    wait_sent(send_b, recv_b, ROWS_B, 1)
    wait_sent(send_v.at[0], recv_v.at[0], ROWS_V, 2)
    wait_sent(send_v.at[1], recv_v.at[1], ROWS_V, 3)
    wait_sent(send_r.at[0], recv_r.at[0], ROWS_V, 4)
    wait_sent(send_r.at[1], recv_r.at[1], ROWS_V, 5)
    res_out.wait()
    upd_out.wait()


def on_device(n, ny, state_field, source, fluid_mask, cell_kind, boundary_side_number, center_matrix,
              flux_jacobian_blocks, wall_matrix, diag_inverse, lower_coupling, upper_neighbour_block):
    planes, comps, rows, lanes = state_field.shape
    assert rows == n and comps == 5 and rows % 8 == 0 and planes % 2 == 0
    cells = comps * rows
    vmem = pltpu.VMEM
    field = vmem((planes, comps, rows, lanes), F32)
    flags = vmem((planes, rows, lanes), jnp.int32)
    blocks = vmem((planes, comps, comps, rows, lanes), F32)
    hbm = pl.BlockSpec(memory_space=pl.ANY)
    smem = pl.BlockSpec(memory_space=pltpu.SMEM)
    out = jax.ShapeDtypeStruct(state_field.shape, F32)
    return pl.pallas_call(
        functools.partial(kernel, n, ny),
        out_shape=(out, out),
        in_specs=[hbm] * 6 + [smem] * 5,
        out_specs=(hbm, hbm),
        scratch_shapes=[
            field, field, flags, flags, flags, blocks,
            vmem(((planes + 2) * cells, lanes), F32),
            vmem((2, planes * comps, lanes), F32),
            vmem((2, planes * comps, lanes), F32),
            vmem((planes * cells, lanes), F32),
            blocks, blocks, blocks, field, field, field, field,
            vmem((n * ROWS_T, lanes), F32), vmem((n * ROWS_T, lanes), F32),
            vmem((n * ROWS_B, lanes), F32), vmem((n * ROWS_B, lanes), F32),
            vmem((2, n * ROWS_V, lanes), F32), vmem((2, n * ROWS_V, lanes), F32),
            vmem((2, n * ROWS_V, lanes), F32), vmem((2, n * ROWS_V, lanes), F32),
            pltpu.SemaphoreType.DMA((6,)), pltpu.SemaphoreType.DMA((2,)),
            pltpu.SemaphoreType.DMA((5,)), pltpu.SemaphoreType.DMA((5,)),
            pltpu.SemaphoreType.DMA((6, n)), pltpu.SemaphoreType.DMA((6, n)),
        ],
        compiler_params=pltpu.CompilerParams(
            collective_id=0, has_side_effects=True, vmem_limit_bytes=48 * 1024 * 1024
        ),
    )(state_field, source, fluid_mask, cell_kind, boundary_side_number, diag_inverse,
      center_matrix, flux_jacobian_blocks, wall_matrix, lower_coupling, upper_neighbour_block)


def solution(mesh):
    field = P("gx", None, "gy", "gz")
    flags = P("gx", "gy", "gz")
    return jax.shard_map(
        functools.partial(on_device, mesh.shape["gx"], mesh.shape["gy"]),
        mesh=mesh,
        in_specs=(field, field, flags, flags, flags, P(), P(), P(), P("gx", None, None, "gy", "gz"), P(), P()),
        out_specs=(field, field),
        check_vma=False,
    )
```

time: 466 us -> 56.7 us (0.12); the launches traced: 459 us -> 55.6 us
  starting transfers between devices: 138 us -> 0 us
  waiting for transfers between devices: 126 us -> 0 us
  other arithmetic: 79.7 us -> 0 us
  matrix products: 67.4 us -> 0 us
  Pallas kernels: 0 us -> 44.9 us
  local copies, waits for them, and re-layouts: 44.1 us -> 10 us
    ppermute x36 -> x0, starting transfers between devices: 138 us -> none  [the longest x30 117 us: shifted(): return lax.ppermute(block, axis, route)]
    ppermute x36 -> x0, waiting for transfers between devices: 126 us -> none  [the longest x30 119 us: shifted(): return lax.ppermute(block, axis, route)]
    dot_general x104 -> x0, matrix products: 67.4 us -> none  [the longest x72 53.3 us: const_apply(): jnp.einsum('ab,...byz->...ayz', matrix, vector, precision=lax.Precision.H...]
    reduce_sum x126 -> x0, other arithmetic: 64.6 us -> none  [the longest x94 61.9 us: volume_operator(): return jnp.sum(blocks * vector[..., None, :, :, :], axis=-3)]
    pallas_call x0 -> x1, Pallas kernels: none -> 44.9 us  [on_device(): pl.pallas_call(functools.partial(kernel, n, ny), out_shape=(out, out), in...]
    while x92 -> x0, local copies, waits for them, and re-layouts: 26.8 us -> none
    sub x32 -> x0, other arithmetic: 10.3 us -> none  [the longest x16 10.1 us: backward(): value - volume_operator(blocks, const_apply(upper_neighbour_block, carry))]
    unnamed x61 -> x21, local copies, waits for them, and re-layouts: 3.12 us -> 10 us
  transfers between devices with their start and end apart: 36 -> 0, of which waited for: 31 -> 0; matrix products, arithmetic and copies ran while one was open for 4% -> 0% of each run, Pallas kernels for 0% -> 0%
where the time goes in v1:
time: 56.7 us; the launch traced here: 55.6 us
  Pallas kernels  44.9 us (79%)
  local copies, waits for them, and re-layouts  10 us (18%)
  between operations  0.65 us (1%)
    pallas_call x1, Pallas kernels, on_device(): pl.pallas_call(functools.partial(kernel, n, ny), out_shape=(out, out), in...  44.9 us
    unnamed x21, local copies, waits for them, and re-layouts  10 us

profile of v1, /device:TPU:32, one launch (start us, length us, event | category | flops | bytes accessed | tf_op | source)
XLA Modules:
  0.0 55.6 jit_solution(2691589786509996417)
XLA Ops:
  0.6 0.7 %copy.13.jac = f32[6,5,5]{2,1,0:T(8,128)S(1)} copy(f32[6,5,5]{2,0,1:T(8,128)} %param.17) | data formatting | bytes 1200 | tf_op args[6]
  1.4 0.0 copy-start
  1.4 1.1 %copy-done = f32[16,5,16,128]{3,2,1,0:T(8,128)S(1)} copy-done((f32[16,5,16,128]{3,2,1,0:T(8,128)S(1)}, f32[16,5,16,128]{3,2,1,0:T(8,128)}, u32[]{:S(2)}) %copy-start) | copy-done | bytes 655384
  2.5 0.0 copy-start.1
  2.5 1.1 %copy-done.1 = f32[16,5,16,128]{3,2,1,0:T(8,128)S(1)} copy-done((f32[16,5,16,128]{3,2,1,0:T(8,128)S(1)}, f32[16,5,16,128]{3,2,1,0:T(8,128)}, u32[]{:S(2)}) %copy-start.1) | copy-done | bytes 655384
  3.5 0.0 copy-start.2
  3.5 0.9 %copy-done.2 = s32[16,16,128]{2,1,0:T(8,128)S(1)} copy-done((s32[16,16,128]{2,1,0:T(8,128)S(1)}, s32[16,16,128]{2,1,0:T(8,128)}, u32[]{:S(2)}) %copy-start.2) | copy-done | bytes 131096
  4.4 0.0 copy-start.3
  4.4 0.9 %copy-done.3 = s32[16,16,128]{2,1,0:T(8,128)S(1)} copy-done((s32[16,16,128]{2,1,0:T(8,128)S(1)}, s32[16,16,128]{2,1,0:T(8,128)}, u32[]{:S(2)}) %copy-start.3) | copy-done | bytes 131096
  5.3 0.0 copy-start.4
  5.4 0.9 %copy-done.4 = s32[16,16,128]{2,1,0:T(8,128)S(1)} copy-done((s32[16,16,128]{2,1,0:T(8,128)S(1)}, s32[16,16,128]{2,1,0:T(8,128)}, u32[]{:S(2)}) %copy-start.4) | copy-done | bytes 131096
  6.3 0.0 copy-start.5
  6.3 0.7 %copy-done.5 = f32[5,5]{1,0:T(8,128)S(1)} copy-done((f32[5,5]{1,0:T(8,128)S(1)}, f32[5,5]{1,0:T(8,128)}, u32[]{:S(2)}) %copy-start.5) | copy-done | bytes 124
  6.9 0.0 copy-start.6
  6.9 0.7 %copy-done.6 = f32[5,5]{1,0:T(8,128)S(1)} copy-done((f32[5,5]{1,0:T(8,128)S(1)}, f32[5,5]{1,0:T(8,128)}, u32[]{:S(2)}) %copy-start.6) | copy-done | bytes 124
  7.6 0.0 copy-start.7
  7.6 0.7 %copy-done.7 = f32[5,5]{1,0:T(8,128)S(1)} copy-done((f32[5,5]{1,0:T(8,128)S(1)}, f32[5,5]{1,0:T(8,128)}, u32[]{:S(2)}) %copy-start.7) | copy-done | bytes 124
  8.3 0.0 copy-start.8
  8.3 0.7 %copy-done.8 = f32[5,5]{1,0:T(8,128)S(1)} copy-done((f32[5,5]{1,0:T(8,128)S(1)}, f32[5,5]{1,0:T(8,128)}, u32[]{:S(2)}) %copy-start.8) | copy-done | bytes 124
  9.0 44.9 %shard_map.122 = (f32[16,5,16,128]{3,2,1,0:T(8,128)S(1)}, f32[16,5,16,128]{3,2,1,0:T(8,128)S(1)}) custom-call(f32[16,5,16,128]{3,2,1,0:T(8,128)S(1)} %copy-done, f32[16,5,16,128]{3,2,1,0:T(8,128)S(1)} %copy-done.1, s32[16,16,128]{2,1,0:T(8,128)S(1)} %copy-done.2, s32[16,16,128]{2,1,0:T(8,128)S(1)} %copy-done.3, s32[16,16,128]{2,1,0:T(8,128)S(1)} %copy-done.4, ...), custom_call_target="tpu_custom_call" | custom-call | tf_op jit(solution)/shard_map/pallas_call | solution.py:346
  53.9 0.8 %copy.16 = f32[16,5,16,128]{3,2,1,0:T(8,128)} copy(f32[16,5,16,128]{3,2,1,0:T(8,128)S(1)} %get-tuple-element.4) | data formatting | bytes 1310720
  54.8 0.8 %copy.17 = f32[16,5,16,128]{3,2,1,0:T(8,128)} copy(f32[16,5,16,128]{3,2,1,0:T(8,128)S(1)} %get-tuple-element.5) | data formatting | bytes 1310720
Async XLA Ops:
  1.4 1.1 %copy-start = (f32[16,5,16,128]{3,2,1,0:T(8,128)S(1)}, f32[16,5,16,128]{3,2,1,0:T(8,128)}, u32[]{:S(2)}) copy-start(f32[16,5,16,128]{3,2,1,0:T(8,128)} %state_hbm.1) | copy-start | bytes 1966084
  2.5 1.1 %copy-start.1 = (f32[16,5,16,128]{3,2,1,0:T(8,128)S(1)}, f32[16,5,16,128]{3,2,1,0:T(8,128)}, u32[]{:S(2)}) copy-start(f32[16,5,16,128]{3,2,1,0:T(8,128)} %source_hbm.1) | copy-start | bytes 1966084
  3.5 0.9 %copy-start.2 = (s32[16,16,128]{2,1,0:T(8,128)S(1)}, s32[16,16,128]{2,1,0:T(8,128)}, u32[]{:S(2)}) copy-start(s32[16,16,128]{2,1,0:T(8,128)} %fluid_hbm.1) | copy-start | bytes 393220
  4.4 0.9 %copy-start.3 = (s32[16,16,128]{2,1,0:T(8,128)S(1)}, s32[16,16,128]{2,1,0:T(8,128)}, u32[]{:S(2)}) copy-start(s32[16,16,128]{2,1,0:T(8,128)} %kind_hbm.1) | copy-start | bytes 393220
  5.3 0.9 %copy-start.4 = (s32[16,16,128]{2,1,0:T(8,128)S(1)}, s32[16,16,128]{2,1,0:T(8,128)}, u32[]{:S(2)}) copy-start(s32[16,16,128]{2,1,0:T(8,128)} %side_hbm.1) | copy-start | bytes 393220
  6.3 0.7 %copy-start.5 = (f32[5,5]{1,0:T(8,128)S(1)}, f32[5,5]{1,0:T(8,128)}, u32[]{:S(2)}) copy-start(f32[5,5]{1,0:T(8,128)} %center.1) | copy-start | bytes 304
  6.9 0.7 %copy-start.6 = (f32[5,5]{1,0:T(8,128)S(1)}, f32[5,5]{1,0:T(8,128)}, u32[]{:S(2)}) copy-start(f32[5,5]{1,0:T(8,128)} %wall.1) | copy-start | bytes 304
  7.6 0.7 %copy-start.7 = (f32[5,5]{1,0:T(8,128)S(1)}, f32[5,5]{1,0:T(8,128)}, u32[]{:S(2)}) copy-start(f32[5,5]{1,0:T(8,128)} %lower.1) | copy-start | bytes 304
  8.3 0.7 %copy-start.8 = (f32[5,5]{1,0:T(8,128)S(1)}, f32[5,5]{1,0:T(8,128)}, u32[]{:S(2)}) copy-start(f32[5,5]{1,0:T(8,128)} %upper.1) | copy-start | bytes 304

commit v2 on v1

v2 whole, which is shorter than its diff:
```python
import functools

import jax
import jax.numpy as jnp
from jax import lax
from jax.experimental import pallas as pl
from jax.experimental.pallas import tpu as pltpu
from jax.sharding import PartitionSpec as P

MESH = pl.DeviceIdType.MESH
F32 = jnp.float32
GROUP = 4
MAPS = 75
ROWS_M = 80
ROWS_V = 16


def aligned(start, size):
    return pl.ds(pl.multiple_of(start, 8), size)


def total(terms):
    terms = list(terms)
    while len(terms) > 1:
        terms = [a + b for a, b in zip(terms[::2], terms[1::2])] + terms[len(terms) & ~1:]
    return terms[0]


def times(block, column):
    return total(part * column[b][None] for b, part in enumerate(block))


def kernel(
    n, ny,
    state_hbm, source_hbm, fluid_hbm, kind_hbm, side_hbm, diag_hbm,
    center, jac, wall, lower, upper,
    update_hbm, residual_hbm,
    state, source, fluid, kind, side, diag,
    masked, ysend, yrecv, zrecv,
    dl, du, tf, g, sw, res, upd,
    send_m1, recv_m1, send_v1, recv_v1, send_r1, recv_r1, left_back,
    send_m2, recv_m2, send_v2, recv_v2, send_r2, recv_r2,
    in_sem, out_sem, halo_send, halo_recv, x_send, x_recv,
):
    planes, comps, rows, lanes = state.shape
    cells = comps * rows
    quarter = rows // GROUP
    me = lax.axis_index("gx")
    my = lax.axis_index("gy")
    mz = lax.axis_index("gz")
    spot, group = lax.rem(me, GROUP), me // GROUP
    east, west = lax.rem(me + 1, n), lax.rem(me + n - 1, n)
    north, south = lax.rem(my + 1, ny), lax.rem(my + ny - 1, ny)
    in_group = [(p, me - spot + p) for p in (lax.rem(spot + k, GROUP) for k in range(1, GROUP))]
    across = [(p, p * GROUP + spot) for p in (lax.rem(group + k, GROUP) for k in range(1, GROUP))]

    pairs = [
        (diag_hbm, diag), (state_hbm, state), (fluid_hbm, fluid), (source_hbm, source), (side_hbm, side), (kind_hbm, kind)
    ]
    loads = [pltpu.make_async_copy(hbm, vmem, in_sem.at[i]) for i, (hbm, vmem) in enumerate(pairs)]
    loads[1].start()
    loads[2].start()
    loads[0].start()

    barrier = pltpu.get_barrier_semaphore()
    for _, peer in in_group + across + [(0, east), (0, west)]:
        pl.semaphore_signal(barrier, inc=1, device_id={"gx": peer}, device_id_type=MESH)
    for other in (north, south):
        pl.semaphore_signal(barrier, inc=1, device_id={"gy": other}, device_id_type=MESH)
    pl.semaphore_signal(barrier, inc=1, device_id={"gz": 1 - mz}, device_id_type=MESH)

    loads[1].wait()
    loads[2].wait()

    def mask_plane(x, _):
        keep = fluid[aligned(x * rows, rows), :].astype(F32)
        for c in range(comps):
            masked[aligned((x + 1) * cells + c * rows, rows), :] = state[x, c] * keep
        return 0

    lax.fori_loop(0, planes, mask_plane, 0)
    ysend[0] = masked[pl.ds(cells + rows - 1, planes * comps, stride=rows), :]
    ysend[1] = masked[pl.ds(cells, planes * comps, stride=rows), :]

    loads[0].wait()
    for i in range(3, 6):
        loads[i].start()

    def products(x, _):
        for a in range(comps):
            row = [diag[x, a, b] for b in range(comps)]
            for c in range(comps):
                dl[x, a, c] = total(row[b] * lower[b, c] for b in range(comps))
                du[x, a, c] = total(row[b] * upper[b, c] for b in range(comps))
        return 0

    lax.fori_loop(0, planes, products, 0)

    def columns(ref, x, half):
        return [ref[x, :, b, aligned(half * 8, 8), :] for b in range(comps)]

    def pack(part, half, held):
        for b in range(comps):
            for a in range(comps):
                for i in range(8 // quarter):
                    send_m1[half * (8 // quarter) + i, part * 25 + b * comps + a] = (
                        held[b][a, i * quarter:(i + 1) * quarter]
                    )

    def forward_maps(half):
        def step(x, held):
            block = columns(dl, x, half)
            held = [times(block, column) for column in held]
            for b in range(comps):
                tf[x, :, b, aligned(half * 8, 8), :] = held[b]
            return held

        first = columns(dl, 0, half)
        for b in range(comps):
            tf[0, :, b, aligned(half * 8, 8), :] = first[b]
        pack(0, half, lax.fori_loop(1, planes, step, first))

    for half in range(rows // 8):
        forward_maps(half)

    def remote(src, dst, send_sem, recv_sem, where):
        return pltpu.make_async_remote_copy(
            src_ref=src, dst_ref=dst, send_sem=send_sem, recv_sem=recv_sem, device_id=where, device_id_type=MESH
        )

    halos = [
        remote(ysend.at[0], yrecv.at[0], halo_send.at[0], halo_recv.at[0], {"gy": north}),
        remote(ysend.at[1], yrecv.at[1], halo_send.at[1], halo_recv.at[1], {"gy": south}),
        remote(
            masked.at[pl.ds(planes * cells, cells)], masked.at[pl.ds(0, cells)],
            halo_send.at[2], halo_recv.at[2], {"gx": east},
        ),
        remote(
            masked.at[pl.ds(cells, cells)], masked.at[pl.ds((planes + 1) * cells, cells)],
            halo_send.at[3], halo_recv.at[3], {"gx": west},
        ),
        remote(masked.at[pl.ds(cells, planes * cells)], zrecv, halo_send.at[4], halo_recv.at[4], {"gz": 1 - mz}),
    ]

    def swap_in_group(src, dst, slot, part):
        return [
            remote(
                src.at[p, part], dst.at[spot, part], x_send.at[slot, k], x_recv.at[slot, k], {"gx": peer}
            )
            for k, (p, peer) in enumerate(in_group)
        ]

    def swap_across(src, dst, size, slot):
        return [
            remote(
                src.at[aligned(p * size, size)], dst.at[aligned(group * size, size)],
                x_send.at[slot, k], x_recv.at[slot, k], {"gx": peer},
            )
            for k, (p, peer) in enumerate(across)
        ]

    maps_a = swap_in_group(send_m1, recv_m1, 0, pl.ds(0, 25))
    maps_b = swap_in_group(send_m1, recv_m1, 1, pl.ds(25, 50))
    maps_2 = swap_across(send_m2, recv_m2, ROWS_M, 2)
    ends_1 = swap_in_group(send_v1, recv_v1, 3, pl.ds(0, 2 * comps))
    ends_2 = swap_across(send_v2, recv_v2, ROWS_V, 4)
    back_2 = swap_across(send_r2, recv_r2, ROWS_V, 5)
    back_1 = swap_in_group(send_r1, recv_r1, 6, pl.ds(0, 2 * comps))

    def start(copies):
        for copy in copies:
            copy.start()

    def arrive(copies):
        for copy in copies:
            copy.wait_recv()

    def keep_own(src, dst, size):
        dst[aligned(group * size, size), :] = src[aligned(group * size, size), :]

    pl.semaphore_wait(barrier, 2 * (GROUP - 1) + 5)
    start(halos)
    start(maps_a)

    def backward_maps(half):
        def through(turn, held):
            x = planes - 2 - turn
            block = columns(du, x, half)
            return [tf[x, :, b, aligned(half * 8, 8), :] - times(block, held[b]) for b in range(comps)]

        def back(turn, held):
            x = planes - 2 - turn
            block = columns(du, x, half)
            return [-times(block, column) for column in held]

        pack(1, half, lax.fori_loop(0, planes - 1, through, columns(tf, planes - 1, half)))
        pack(2, half, lax.fori_loop(0, planes - 1, back, [-column for column in columns(du, planes - 1, half)]))

    for half in range(rows // 8):
        backward_maps(half)
    start(maps_b)
    recv_m1[spot] = send_m1[spot]

    arrive(halos[2:])
    masked[0:cells, :] = jnp.where(me == 0, 0.0, masked[0:cells, :])
    top = pl.ds((planes + 1) * cells, cells)
    masked[top, :] = jnp.where(me == n - 1, 0.0, masked[top, :])
    for i in range(3, 6):
        loads[i].wait()

    row_id = lax.broadcasted_iota(jnp.int32, (rows, lanes), 0)
    lane_id = lax.broadcasted_iota(jnp.int32, (rows, lanes), 1)
    from_low = jnp.where(mz == 0, 0.0, 1.0).astype(F32)
    from_high = 1.0 - from_low

    def weights(flag, wet):
        return jnp.where(flag == 0, 1.0, jnp.where(flag == 1, 2.0, 4.0)) * wet.astype(F32)

    def residual_planes(step, _):
        xs = (2 * step, 2 * step + 1)
        sides = [side[aligned(x * rows, rows), :] for x in xs]
        flux = [[None] * comps for _ in xs]

        def add(matrix, b, values):
            for a in range(comps):
                weight = matrix(a, b)
                for i, value in enumerate(values):
                    term = weight * value
                    flux[i][a] = term if flux[i][a] is None else flux[i][a] + term

        for b in range(comps):
            own = [state[x, b] for x in xs]
            add(lambda a, b: center[a, b], b, own)
            add(lambda a, b: wall[a, b], b, [jnp.where(s < 6, v, 0.0) for s, v in zip(sides, own)])
            here = [masked[aligned((x + 1) * cells + b * rows, rows), :] for x in xs]
            other = [zrecv[aligned(x * cells + b * rows, rows), :] for x in xs]
            neighbours = [
                [masked[aligned(x * cells + b * rows, rows), :] for x in xs],
                [masked[aligned((x + 2) * cells + b * rows, rows), :] for x in xs],
                [pltpu.roll(v, 1, 0) for v in here],
                [pltpu.roll(v, rows - 1, 0) for v in here],
                [pltpu.roll(jnp.where(lane_id == lanes - 1, o * from_low, v), 1, 1) for o, v in zip(other, here)],
                [pltpu.roll(jnp.where(lane_id == 0, o * from_high, v), lanes - 1, 1) for o, v in zip(other, here)],
            ]
            edge = [None, None, 0, rows - 1, None, None]
            for d in range(6):
                closed = [s == d for s in sides]
                if edge[d] is not None:
                    closed = [jnp.logical_or(c, row_id == edge[d]) for c in closed]
                add(lambda a, b: jac[a, d, b], b, [jnp.where(c, 0.0, v) for c, v in zip(closed, neighbours[d])])
        for i, x in enumerate(xs):
            weight = weights(kind[aligned(x * rows, rows), :], fluid[aligned(x * rows, rows), :])
            for a in range(comps):
                res[aligned(x * cells + a * rows, rows), :] = (source[x, a] - flux[i][a]) * weight
        return 0

    lax.fori_loop(0, planes // 2, residual_planes, 0)

    arrive(halos[:2])
    for i, (d, row) in enumerate(((2, 0), (3, rows - 1))):
        edge_rows = pl.ds(row, planes, stride=rows)
        is_open = jnp.logical_and(side[edge_rows, :] != d, my != (0, ny - 1)[i])
        weight = jnp.where(is_open, weights(kind[edge_rows, :], fluid[edge_rows, :]), 0.0)
        beyond = [yrecv[i, pl.ds(b, planes, stride=comps), :] for b in range(comps)]
        for a in range(comps):
            at = pl.ds(a * rows + row, planes, stride=cells)
            res[at, :] = res[at, :] - weight * total(jac[a, d, b] * beyond[b] for b in range(comps))
    res_out = pltpu.make_async_copy(res, residual_hbm, out_sem.at[0])
    res_out.start()

    def first_forward(x, held):
        terms = [res[aligned(x * cells + b * rows, rows), :] for b in range(comps)]
        for a in range(comps):
            g[x, a] = total(diag[x, a, b] * terms[b] for b in range(comps))
        return forward(x, held)

    def forward(x, held):
        held = [
            g[x, a] + total(dl[x, a, b] * held[b] for b in range(comps)) for a in range(comps)
        ]
        for a in range(comps):
            sw[x, a] = held[a]
        return held

    def backward(turn, held):
        x = planes - 1 - turn
        return [
            sw[x, a] - total(du[x, a, b] * held[b] for b in range(comps)) for a in range(comps)
        ]

    zeros = [jnp.zeros((rows, lanes), F32)] * comps
    east_end = lax.fori_loop(0, planes, first_forward, zeros)
    west_end = lax.fori_loop(0, planes, backward, zeros)
    for c, value in enumerate(list(east_end) + list(west_end)):
        for i in range(GROUP):
            send_v1[i, c] = value[i * quarter:(i + 1) * quarter]
    start(ends_1)
    recv_v1[spot] = send_v1[spot]

    def held_map(d, part):
        return [recv_m1[d, pl.ds(part * 25 + b * comps, comps)] for b in range(comps)]

    arrive(maps_a)
    arrive(maps_b)
    ahead, through, behind = [held_map(0, part) for part in range(3)]
    for d in range(1, GROUP):
        for b in range(comps):
            left_back[d, pl.ds(b * comps, comps)] = behind[b]
        own_through = held_map(d, 1)
        turned = [times(own_through, column) for column in ahead]
        through = [through[b] + times(behind, turned[b]) for b in range(comps)]
        own_ahead = held_map(d, 0)
        ahead = [times(own_ahead, column) for column in ahead]
        behind = [times(behind, column) for column in held_map(d, 2)]
    for part, columns_of in enumerate((ahead, through, behind)):
        for b in range(comps):
            for a in range(comps):
                send_m2[pl.ds(part * 25 + a * comps + b, GROUP, stride=ROWS_M), :] = columns_of[b][a]
    start(maps_2)
    keep_own(send_m2, recv_m2, ROWS_M)

    arrive(ends_1)
    forward_end = recv_v1[0, pl.ds(0, comps)]
    backward_end = recv_v1[0, pl.ds(comps, comps)]
    for d in range(1, GROUP):
        turned = recv_v1[d, pl.ds(comps, comps)] + times(held_map(d, 1), forward_end)
        left = [left_back[d, pl.ds(b * comps, comps)] for b in range(comps)]
        backward_end = backward_end + times(left, turned)
        forward_end = recv_v1[d, pl.ds(0, comps)] + times(held_map(d, 0), forward_end)
    for c in range(comps):
        send_v2[pl.ds(c, GROUP, stride=ROWS_V), :] = forward_end[c]
        send_v2[pl.ds(8 + c, GROUP, stride=ROWS_V), :] = backward_end[c]
    start(ends_2)
    keep_own(send_v2, recv_v2, ROWS_V)

    def apply(start_row, vector):
        return total(
            recv_m2[pl.ds(start_row + b, comps, stride=comps), :] * vector[b:b + 1] for b in range(comps)
        )

    arrive(maps_2)
    arrive(ends_2)
    came = jnp.zeros((comps, lanes), F32)
    forward_in = []
    for i in range(GROUP):
        forward_in.append(came)
        send_r2[pl.ds(i * ROWS_V, comps), :] = came
        if i < GROUP - 1:
            came = recv_v2[pl.ds(i * ROWS_V, comps), :] + apply(i * ROWS_M, came)
    came = jnp.zeros((comps, lanes), F32)
    for i in range(GROUP - 1, -1, -1):
        send_r2[pl.ds(i * ROWS_V + 8, comps), :] = came
        if i > 0:
            came = (
                recv_v2[pl.ds(i * ROWS_V + 8, comps), :] + apply(i * ROWS_M + 25, forward_in[i])
                + apply(i * ROWS_M + 50, came)
            )
    start(back_2)
    keep_own(send_r2, recv_r2, ROWS_V)

    arrive(back_2)
    came = jnp.stack([recv_r2[pl.ds(c, GROUP, stride=ROWS_V), :] for c in range(comps)])
    forward_in = []
    for d in range(GROUP):
        forward_in.append(came)
        send_r1[d, pl.ds(0, comps)] = came
        if d < GROUP - 1:
            came = recv_v1[d, pl.ds(0, comps)] + times(held_map(d, 0), came)
    came = jnp.stack([recv_r2[pl.ds(8 + c, GROUP, stride=ROWS_V), :] for c in range(comps)])
    for d in range(GROUP - 1, -1, -1):
        send_r1[d, pl.ds(comps, comps)] = came
        if d > 0:
            came = (
                recv_v1[d, pl.ds(comps, comps)] + times(held_map(d, 1), forward_in[d]) + times(held_map(d, 2), came)
            )
    start(back_1)
    recv_r1[spot] = send_r1[spot]

    arrive(back_1)
    came = [
        jnp.concatenate([recv_r1[i, c] for i in range(GROUP)], axis=0) for c in range(2 * comps)
    ]
    lax.fori_loop(0, planes, forward, came[:comps])

    def finish(turn, held):
        x = planes - 1 - turn
        held = backward(turn, held)
        for a in range(comps):
            upd[x, a] = held[a]
        return held

    lax.fori_loop(0, planes, finish, came[comps:])
    upd_out = pltpu.make_async_copy(upd, update_hbm, out_sem.at[1])
    upd_out.start()
    for copy in halos + maps_a + maps_b + maps_2 + ends_1 + ends_2 + back_2 + back_1:
        copy.wait_send()
    res_out.wait()
    upd_out.wait()


def on_device(n, ny, state_field, source, fluid_mask, cell_kind, boundary_side_number, center_matrix,
              flux_jacobian_blocks, wall_matrix, diag_inverse, lower_coupling, upper_neighbour_block):
    planes, comps, rows, lanes = state_field.shape
    assert n == GROUP * GROUP and rows == n and comps == 5 and planes % 2 == 0
    cells = comps * rows
    quarter = rows // GROUP
    vmem = pltpu.VMEM
    field = vmem((planes, comps, rows, lanes), F32)
    flags = vmem((planes * rows, lanes), jnp.int32)
    blocks = vmem((planes, comps, comps, rows, lanes), F32)
    maps = vmem((GROUP, MAPS, quarter, lanes), F32)
    ends = vmem((GROUP, 2 * comps, quarter, lanes), F32)
    maps_across = vmem((GROUP * ROWS_M, lanes), F32)
    ends_across = vmem((GROUP * ROWS_V, lanes), F32)
    hbm = pl.BlockSpec(memory_space=pl.ANY)
    smem = pl.BlockSpec(memory_space=pltpu.SMEM)
    update, residual = pl.pallas_call(
        functools.partial(kernel, n, ny),
        out_shape=(
            jax.ShapeDtypeStruct(state_field.shape, F32),
            jax.ShapeDtypeStruct((planes * cells, lanes), F32),
        ),
        in_specs=[hbm] * 6 + [smem] * 5,
        out_specs=(hbm, hbm),
        scratch_shapes=[
            field, field, flags, flags, flags, blocks,
            vmem(((planes + 2) * cells, lanes), F32),
            vmem((2, planes * comps, lanes), F32),
            vmem((2, planes * comps, lanes), F32),
            vmem((planes * cells, lanes), F32),
            blocks, blocks, blocks, field, field, vmem((planes * cells, lanes), F32), field,
            maps, maps, ends, ends, ends, ends, vmem((GROUP, 25, quarter, lanes), F32),
            maps_across, maps_across, ends_across, ends_across, ends_across, ends_across,
            pltpu.SemaphoreType.DMA((6,)), pltpu.SemaphoreType.DMA((2,)),
            pltpu.SemaphoreType.DMA((5,)), pltpu.SemaphoreType.DMA((5,)),
            pltpu.SemaphoreType.DMA((7, GROUP - 1)), pltpu.SemaphoreType.DMA((7, GROUP - 1)),
        ],
        compiler_params=pltpu.CompilerParams(
            collective_id=0, has_side_effects=True, vmem_limit_bytes=63 * 1024 * 1024
        ),
    )(
        state_field, source, *(a.reshape(planes * rows, lanes) for a in (fluid_mask, cell_kind, boundary_side_number)),
        diag_inverse, center_matrix, jnp.transpose(flux_jacobian_blocks, (1, 0, 2)), wall_matrix,
        lower_coupling, upper_neighbour_block,
    )
    return update, residual.reshape(state_field.shape)


def solution(mesh):
    field = P("gx", None, "gy", "gz")
    flags = P("gx", "gy", "gz")
    return jax.shard_map(
        functools.partial(on_device, mesh.shape["gx"], mesh.shape["gy"]),
        mesh=mesh,
        in_specs=(field, field, flags, flags, flags, P(), P(), P(), P("gx", None, None, "gy", "gz"), P(), P()),
        out_specs=(field, field),
        check_vma=False,
    )
```

time: 56.7 us -> 43.5 us (0.77); the launches traced: 55.6 us -> 43.3 us
  Pallas kernels: 44.9 us -> 38.7 us
  local copies, waits for them, and re-layouts: 10 us -> 3.93 us
    pallas_call x1, Pallas kernels: 44.9 us -> 38.7 us  [on_device(): pl.pallas_call(functools.partial(kernel, n, ny), out_shape=(jax.ShapeDtyp...]
    unnamed x21 -> x2, local copies, waits for them, and re-layouts: 10 us -> 3.93 us
where the time goes in v2:
time: 43.5 us; the launch traced here: 43.3 us
  Pallas kernels  38.7 us (89%)
  local copies, waits for them, and re-layouts  3.93 us (9%)
  between operations  0.64 us (1%)
    pallas_call x1, Pallas kernels, on_device(): pl.pallas_call(functools.partial(kernel, n, ny), out_shape=(jax.ShapeDtyp...  38.7 us
    unnamed x2, local copies, waits for them, and re-layouts  3.93 us

profile of v2, /device:TPU:32, one launch (start us, length us, event | category | flops | bytes accessed | tf_op | source)
XLA Modules:
  0.0 43.3 jit_solution(10529400452162737341)
XLA Ops:
  0.6 38.7 %shard_map.122 = (f32[16,5,16,128]{3,2,1,0:T(8,128)}, f32[1280,128]{1,0:T(8,128)}) custom-call(f32[16,5,16,128]{3,2,1,0:T(8,128)} %state_hbm.1, f32[16,5,16,128]{3,2,1,0:T(8,128)} %source_hbm.1, s32[256,128]{1,0:T(8,128)} %bitcast.6, s32[256,128]{1,0:T(8,128)} %bitcast.7, s32[256,128]{1,0:T(8,128)} %bitcast.8, f32[16,5,5,16,128]{4,3,2,1,0:T(8,128)} %diag_hbm.1, ...), custom_call_target="tpu_custom_call" | custom-call | tf_op jit(solution)/shard_map/pallas_call | solution.py:417
  39.3 2.0 %copy.15 = f32[16,5,16,128]{3,2,1,0:T(8,128)} copy(f32[16,5,16,128]{3,2,1,0:T(8,128)} %get-tuple-element.8) | data formatting | bytes 1310720
  41.3 2.0 %copy.16 = f32[16,5,16,128]{3,2,1,0:T(8,128)} copy(f32[16,5,16,128]{3,2,1,0:T(8,128)} %bitcast.5) | data formatting | bytes 1310720

commit v3 on v2

--- a/solution.py
+++ b/solution.py
@@ -34,13 +34,13 @@
     n, ny,
     state_hbm, source_hbm, fluid_hbm, kind_hbm, side_hbm, diag_hbm,
     center, jac, wall, lower, upper,
-    update_hbm, residual_hbm,
+    upd, res,
     state, source, fluid, kind, side, diag,
     masked, ysend, yrecv, zrecv,
-    dl, du, tf, g, sw, res, upd,
+    dl, du, tf, g, sw,
     send_m1, recv_m1, send_v1, recv_v1, send_r1, recv_r1, left_back,
     send_m2, recv_m2, send_v2, recv_v2, send_r2, recv_r2,
-    in_sem, out_sem, halo_send, halo_recv, x_send, x_recv,
+    in_sem, halo_send, halo_recv, x_send, x_recv,
 ):
     planes, comps, rows, lanes = state.shape
     cells = comps * rows
@@ -265,8 +265,6 @@
         for a in range(comps):
             at = pl.ds(a * rows + row, planes, stride=cells)
             res[at, :] = res[at, :] - weight * total(jac[a, d, b] * beyond[b] for b in range(comps))
-    res_out = pltpu.make_async_copy(res, residual_hbm, out_sem.at[0])
-    res_out.start()
 
     def first_forward(x, held):
         terms = [res[aligned(x * cells + b * rows, rows), :] for b in range(comps)]
@@ -390,12 +388,8 @@
         return held
 
     lax.fori_loop(0, planes, finish, came[comps:])
-    upd_out = pltpu.make_async_copy(upd, update_hbm, out_sem.at[1])
-    upd_out.start()
     for copy in halos + maps_a + maps_b + maps_2 + ends_1 + ends_2 + back_2 + back_1:
         copy.wait_send()
-    res_out.wait()
-    upd_out.wait()
 
 
 def on_device(n, ny, state_field, source, fluid_mask, cell_kind, boundary_side_number, center_matrix,
@@ -412,38 +406,60 @@
     ends = vmem((GROUP, 2 * comps, quarter, lanes), F32)
     maps_across = vmem((GROUP * ROWS_M, lanes), F32)
     ends_across = vmem((GROUP * ROWS_V, lanes), F32)
-    hbm = pl.BlockSpec(memory_space=pl.ANY)
+    hbm = pl.BlockSpec(memory_space=pltpu.HBM)
     smem = pl.BlockSpec(memory_space=pltpu.SMEM)
     update, residual = pl.pallas_call(
         functools.partial(kernel, n, ny),
         out_shape=(
-            jax.ShapeDtypeStruct(state_field.shape, F32),
-            jax.ShapeDtypeStruct((planes * cells, lanes), F32),
+            pltpu.VMEM(state_field.shape, F32),
+            pltpu.VMEM((planes * cells, lanes), F32),
         ),
         in_specs=[hbm] * 6 + [smem] * 5,
-        out_specs=(hbm, hbm),
+        out_specs=(pl.BlockSpec(memory_space=pltpu.VMEM),) * 2,
         scratch_shapes=[
             field, field, flags, flags, flags, blocks,
             vmem(((planes + 2) * cells, lanes), F32),
             vmem((2, planes * comps, lanes), F32),
             vmem((2, planes * comps, lanes), F32),
             vmem((planes * cells, lanes), F32),
-            blocks, blocks, blocks, field, field, vmem((planes * cells, lanes), F32), field,
+            blocks, blocks, blocks, field, field,
             maps, maps, ends, ends, ends, ends, vmem((GROUP, 25, quarter, lanes), F32),
             maps_across, maps_across, ends_across, ends_across, ends_across, ends_across,
-            pltpu.SemaphoreType.DMA((6,)), pltpu.SemaphoreType.DMA((2,)),
+            pltpu.SemaphoreType.DMA((6,)),
             pltpu.SemaphoreType.DMA((5,)), pltpu.SemaphoreType.DMA((5,)),
             pltpu.SemaphoreType.DMA((7, GROUP - 1)), pltpu.SemaphoreType.DMA((7, GROUP - 1)),
         ],
         compiler_params=pltpu.CompilerParams(
-            collective_id=0, has_side_effects=True, vmem_limit_bytes=63 * 1024 * 1024
+            collective_id=0, has_side_effects=True, vmem_limit_bytes=61 * 1024 * 1024
         ),
     )(
         state_field, source, *(a.reshape(planes * rows, lanes) for a in (fluid_mask, cell_kind, boundary_side_number)),
         diag_inverse, center_matrix, jnp.transpose(flux_jacobian_blocks, (1, 0, 2)), wall_matrix,
         lower_coupling, upper_neighbour_block,
     )
-    return update, residual.reshape(state_field.shape)
+    return write(update, residual.reshape(state_field.shape))
+
+
+def write_kernel(update, residual, update_out, residual_out, sems):
+    copies = [
+        pltpu.make_async_copy(update, update_out, sems.at[0]),
+        pltpu.make_async_copy(residual, residual_out, sems.at[1]),
+    ]
+    for copy in copies:
+        copy.start()
+    for copy in copies:
+        copy.wait()
+
+
+def write(update, residual):
+    return pl.pallas_call(
+        write_kernel,
+        out_shape=(jax.ShapeDtypeStruct(update.shape, F32), jax.ShapeDtypeStruct(residual.shape, F32)),
+        in_specs=[pl.BlockSpec(memory_space=pltpu.VMEM)] * 2,
+        out_specs=(pl.BlockSpec(memory_space=pltpu.HBM),) * 2,
+        scratch_shapes=[pltpu.SemaphoreType.DMA((2,))],
+        compiler_params=pltpu.CompilerParams(vmem_limit_bytes=1024 * 1024),
+    )(update, residual)
 
 
 def solution(mesh):

time: 43.5 us -> 39.8 us (0.915)
  local copies, waits for them, and re-layouts: 3.93 us -> 0 us
    unnamed x2 -> x0, local copies, waits for them, and re-layouts: 3.93 us -> none
    pallas_call x1 -> x2, Pallas kernels: 38.7 us -> 38.9 us  [the longest x1 37.8 us: on_device(): pl.pallas_call(functools.partial(kernel, n, ny), out_shape=(pltpu.VMEM(st...]
where the time goes in v3:
time: 39.8 us; the launch traced here: 39.6 us
  Pallas kernels  38.9 us (98%)
  between operations  0.64 us (2%)
    pallas_call x1, Pallas kernels, on_device(): pl.pallas_call(functools.partial(kernel, n, ny), out_shape=(pltpu.VMEM(st...  37.8 us
    pallas_call x1, Pallas kernels, write(): pl.pallas_call(write_kernel, out_shape=(jax.ShapeDtypeStruct(update.shape...  1.07 us

profile of v3, /device:TPU:32, one launch (start us, length us, event | category | flops | bytes accessed | tf_op | source)
XLA Modules:
  0.0 39.6 jit_solution(4893891072482468987)
XLA Ops:
  0.6 37.8 %shard_map.122 = (f32[16,5,16,128]{3,2,1,0:T(8,128)S(1)}, f32[1280,128]{1,0:T(8,128)S(1)}) custom-call(f32[16,5,16,128]{3,2,1,0:T(8,128)} %state_hbm.1, f32[16,5,16,128]{3,2,1,0:T(8,128)} %source_hbm.1, s32[256,128]{1,0:T(8,128)} %bitcast.6, s32[256,128]{1,0:T(8,128)} %bitcast.7, s32[256,128]{1,0:T(8,128)} %bitcast.8, f32[16,5,5,16,128]{4,3,2,1,0:T(8,128)} %diag_hbm.1, ...), custom_call_target="tpu_custom_call" | custom-call | tf_op jit(solution)/shard_map/pallas_call | solution.py:411
  38.5 1.1 %shard_map.123 = (f32[16,5,16,128]{3,2,1,0:T(8,128)}, f32[16,5,16,128]{3,2,1,0:T(8,128)}) custom-call(f32[16,5,16,128]{3,2,1,0:T(8,128)S(1)} %get-tuple-element.4.update, f32[16,5,16,128]{3,2,1,0:T(8,128)S(1)} %bitcast.5), custom_call_target="tpu_custom_call" | custom-call | tf_op jit(solution)/shard_map/pallas_call | solution.py:455

commit v4 on v3

--- a/solution.py
+++ b/solution.py
@@ -33,8 +33,9 @@
 def kernel(
     n, ny,
     state_hbm, source_hbm, fluid_hbm, kind_hbm, side_hbm, diag_hbm,
+    center_hbm, jac_hbm, wall_hbm, lower_hbm, upper_hbm,
+    upd, res,
     center, jac, wall, lower, upper,
-    upd, res,
     state, source, fluid, kind, side, diag,
     masked, ysend, yrecv, zrecv,
     dl, du, tf, g, sw,
@@ -55,19 +56,18 @@
     across = [(p, p * GROUP + spot) for p in (lax.rem(group + k, GROUP) for k in range(1, GROUP))]
 
     pairs = [
-        (diag_hbm, diag), (state_hbm, state), (fluid_hbm, fluid), (source_hbm, source), (side_hbm, side), (kind_hbm, kind)
+        (diag_hbm, diag), (state_hbm, state), (fluid_hbm, fluid), (source_hbm, source), (side_hbm, side), (kind_hbm, kind),
+        (lower_hbm, lower), (upper_hbm, upper), (center_hbm, center), (wall_hbm, wall), (jac_hbm, jac),
     ]
     loads = [pltpu.make_async_copy(hbm, vmem, in_sem.at[i]) for i, (hbm, vmem) in enumerate(pairs)]
-    loads[1].start()
-    loads[2].start()
-    loads[0].start()
-
     barrier = pltpu.get_barrier_semaphore()
-    for _, peer in in_group + across + [(0, east), (0, west)]:
-        pl.semaphore_signal(barrier, inc=1, device_id={"gx": peer}, device_id_type=MESH)
     for other in (north, south):
         pl.semaphore_signal(barrier, inc=1, device_id={"gy": other}, device_id_type=MESH)
+    for _, peer in [(0, east), (0, west)] + across + in_group:
+        pl.semaphore_signal(barrier, inc=1, device_id={"gx": peer}, device_id_type=MESH)
     pl.semaphore_signal(barrier, inc=1, device_id={"gz": 1 - mz}, device_id_type=MESH)
+    for i in (1, 2, 6, 7, 0, 8, 9, 10):
+        loads[i].start()
 
     loads[1].wait()
     loads[2].wait()
@@ -82,7 +82,8 @@
     ysend[0] = masked[pl.ds(cells + rows - 1, planes * comps, stride=rows), :]
     ysend[1] = masked[pl.ds(cells, planes * comps, stride=rows), :]
 
-    loads[0].wait()
+    for i in (6, 7, 0):
+        loads[i].wait()
     for i in range(3, 6):
         loads[i].start()
 
@@ -205,7 +206,7 @@
     masked[0:cells, :] = jnp.where(me == 0, 0.0, masked[0:cells, :])
     top = pl.ds((planes + 1) * cells, cells)
     masked[top, :] = jnp.where(me == n - 1, 0.0, masked[top, :])
-    for i in range(3, 6):
+    for i in (3, 4, 5, 8, 9, 10):
         loads[i].wait()
 
     row_id = lax.broadcasted_iota(jnp.int32, (rows, lanes), 0)
@@ -407,16 +408,17 @@
     maps_across = vmem((GROUP * ROWS_M, lanes), F32)
     ends_across = vmem((GROUP * ROWS_V, lanes), F32)
     hbm = pl.BlockSpec(memory_space=pltpu.HBM)
-    smem = pl.BlockSpec(memory_space=pltpu.SMEM)
+    matrix = pltpu.SMEM((comps, comps), F32)
     update, residual = pl.pallas_call(
         functools.partial(kernel, n, ny),
         out_shape=(
             pltpu.VMEM(state_field.shape, F32),
             pltpu.VMEM((planes * cells, lanes), F32),
         ),
-        in_specs=[hbm] * 6 + [smem] * 5,
+        in_specs=[hbm] * 11,
         out_specs=(pl.BlockSpec(memory_space=pltpu.VMEM),) * 2,
         scratch_shapes=[
+            matrix, pltpu.SMEM((comps, 6, comps), F32), matrix, matrix, matrix,
             field, field, flags, flags, flags, blocks,
             vmem(((planes + 2) * cells, lanes), F32),
             vmem((2, planes * comps, lanes), F32),
@@ -425,7 +427,7 @@
             blocks, blocks, blocks, field, field,
             maps, maps, ends, ends, ends, ends, vmem((GROUP, 25, quarter, lanes), F32),
             maps_across, maps_across, ends_across, ends_across, ends_across, ends_across,
-            pltpu.SemaphoreType.DMA((6,)),
+            pltpu.SemaphoreType.DMA((11,)),
             pltpu.SemaphoreType.DMA((5,)), pltpu.SemaphoreType.DMA((5,)),
             pltpu.SemaphoreType.DMA((7, GROUP - 1)), pltpu.SemaphoreType.DMA((7, GROUP - 1)),
         ],

time: 39.8 us -> 38.5 us (0.967)
  Pallas kernels: 38.9 us -> 37.7 us
    pallas_call x1, Pallas kernels: 37.8 us -> 36.6 us  [on_device(): pl.pallas_call(functools.partial(kernel, n, ny), out_shape=(pltpu.VMEM(st...]
where the time goes in v4:
time: 38.5 us; the launch traced here: 38.4 us
  Pallas kernels  37.7 us (98%)
  between operations  0.64 us (2%)
    pallas_call x1, Pallas kernels, on_device(): pl.pallas_call(functools.partial(kernel, n, ny), out_shape=(pltpu.VMEM(st...  36.6 us
    pallas_call x1, Pallas kernels, write(): pl.pallas_call(write_kernel, out_shape=(jax.ShapeDtypeStruct(update.shape...  1.07 us

profile of v4, /device:TPU:32, one launch (start us, length us, event | category | flops | bytes accessed | tf_op | source)
XLA Modules:
  0.0 38.4 jit_solution(9729336993834602028)
XLA Ops:
  0.6 36.6 %shard_map.122 = (f32[16,5,16,128]{3,2,1,0:T(8,128)S(1)}, f32[1280,128]{1,0:T(8,128)S(1)}) custom-call(f32[16,5,16,128]{3,2,1,0:T(8,128)} %state_hbm.1, f32[16,5,16,128]{3,2,1,0:T(8,128)} %source_hbm.1, s32[256,128]{1,0:T(8,128)} %bitcast.6, s32[256,128]{1,0:T(8,128)} %bitcast.7, s32[256,128]{1,0:T(8,128)} %bitcast.8, f32[16,5,5,16,128]{4,3,2,1,0:T(8,128)} %diag_hbm.1, ...), custom_call_target="tpu_custom_call" | custom-call | tf_op jit(solution)/shard_map/pallas_call | solution.py:412
  37.3 1.1 %shard_map.123 = (f32[16,5,16,128]{3,2,1,0:T(8,128)}, f32[16,5,16,128]{3,2,1,0:T(8,128)}) custom-call(f32[16,5,16,128]{3,2,1,0:T(8,128)S(1)} %get-tuple-element.4.update, f32[16,5,16,128]{3,2,1,0:T(8,128)S(1)} %bitcast.5), custom_call_target="tpu_custom_call" | custom-call | tf_op jit(solution)/shard_map/pallas_call | solution.py:457

commit v5 on v4

--- a/solution.py
+++ b/solution.py
@@ -39,9 +39,9 @@
     state, source, fluid, kind, side, diag,
     masked, ysend, yrecv, zrecv,
     dl, du, tf, g, sw,
-    send_m1, recv_m1, send_v1, recv_v1, send_r1, recv_r1, left_back,
+    send_m1, recv_m1, send_v1, recv_v1, send_r1, recv_r1, send_mr, recv_mr,
     send_m2, recv_m2, send_v2, recv_v2, send_r2, recv_r2,
-    in_sem, halo_send, halo_recv, x_send, x_recv,
+    in_sem, halo_send, halo_recv, x_send, x_recv, line_send, line_recv,
 ):
     planes, comps, rows, lanes = state.shape
     cells = comps * rows
@@ -53,6 +53,7 @@
     east, west = lax.rem(me + 1, n), lax.rem(me + n - 1, n)
     north, south = lax.rem(my + 1, ny), lax.rem(my + ny - 1, ny)
     in_group = [(p, me - spot + p) for p in (lax.rem(spot + k, GROUP) for k in range(1, GROUP))]
+    line = [lax.rem(me + k, n) for k in range(1, n)]
     across = [(p, p * GROUP + spot) for p in (lax.rem(group + k, GROUP) for k in range(1, GROUP))]
 
     pairs = [
@@ -63,7 +64,7 @@
     barrier = pltpu.get_barrier_semaphore()
     for other in (north, south):
         pl.semaphore_signal(barrier, inc=1, device_id={"gy": other}, device_id_type=MESH)
-    for _, peer in [(0, east), (0, west)] + across + in_group:
+    for peer in line:
         pl.semaphore_signal(barrier, inc=1, device_id={"gx": peer}, device_id_type=MESH)
     pl.semaphore_signal(barrier, inc=1, device_id={"gz": 1 - mz}, device_id_type=MESH)
     for i in (1, 2, 6, 7, 0, 8, 9, 10):
@@ -165,13 +166,34 @@
     maps_2 = swap_across(send_m2, recv_m2, ROWS_M, 2)
     ends_1 = swap_in_group(send_v1, recv_v1, 3, pl.ds(0, 2 * comps))
     ends_2 = swap_across(send_v2, recv_v2, ROWS_V, 4)
-    back_2 = swap_across(send_r2, recv_r2, ROWS_V, 5)
+    maps_p = swap_in_group(send_mr, recv_mr, 5, pl.ds(0, 25))
+    maps_q = swap_in_group(send_mr, recv_mr, 7, pl.ds(25, 50))
+    mine = spot * GROUP + group
+    back_2 = [
+        remote(
+            send_r2.at[aligned(peer // GROUP * ROWS_V, ROWS_V)], recv_r2.at[aligned(mine * ROWS_V, ROWS_V)],
+            line_send.at[k], line_recv.at[k], {"gx": peer},
+        )
+        for k, peer in enumerate(line)
+    ]
     back_1 = swap_in_group(send_r1, recv_r1, 6, pl.ds(0, 2 * comps))
 
     def start(copies):
         for copy in copies:
             copy.start()
 
+    def start_but(copies, skipped):
+        for (p, _), copy in zip(in_group, copies):
+            pl.when(p != skipped)(copy.start)
+
+    def sent_but(copies, skipped):
+        for (p, _), copy in zip(in_group, copies):
+            pl.when(p != skipped)(copy.wait_send)
+
+    def arrive_but(copies, skipped):
+        for copy in copies:
+            pl.when(spot != skipped)(copy.wait_recv)
+
     def arrive(copies):
         for copy in copies:
             copy.wait_recv()
@@ -179,7 +201,7 @@
     def keep_own(src, dst, size):
         dst[aligned(group * size, size), :] = src[aligned(group * size, size), :]
 
-    pl.semaphore_wait(barrier, 2 * (GROUP - 1) + 5)
+    pl.semaphore_wait(barrier, n + 2)
     start(halos)
     start(maps_a)
 
@@ -299,38 +321,92 @@
     def held_map(d, part):
         return [recv_m1[d, pl.ds(part * 25 + b * comps, comps)] for b in range(comps)]
 
+    ones = jnp.ones((quarter, lanes), F32)
+    same = [jnp.stack([ones if a == b else 0.0 * ones for a in range(comps)]) for b in range(comps)]
+
+    def chain(block, other):
+        return [times(block, column) for column in other]
+
+    def join(first, second):
+        return [a + b for a, b in zip(first, second)]
+
+    def put(d, part, other):
+        for b in range(comps):
+            send_mr[d, pl.ds(part * 25 + b * comps, comps)] = other[b]
+
+    def put_across(part, other):
+        for b in range(comps):
+            for a in range(comps):
+                send_m2[pl.ds(part * 25 + a * comps + b, GROUP, stride=ROWS_M), :] = other[b][a]
+
     arrive(maps_a)
     arrive(maps_b)
-    ahead, through, behind = [held_map(0, part) for part in range(3)]
+    last = GROUP - 1
+    ahead = held_map(0, 0)
+    put(1, 0, ahead)
     for d in range(1, GROUP):
-        for b in range(comps):
-            left_back[d, pl.ds(b * comps, comps)] = behind[b]
-        own_through = held_map(d, 1)
-        turned = [times(own_through, column) for column in ahead]
-        through = [through[b] + times(behind, turned[b]) for b in range(comps)]
-        own_ahead = held_map(d, 0)
-        ahead = [times(own_ahead, column) for column in ahead]
-        behind = [times(behind, column) for column in held_map(d, 2)]
-    for part, columns_of in enumerate((ahead, through, behind)):
-        for b in range(comps):
-            for a in range(comps):
-                send_m2[pl.ds(part * 25 + a * comps + b, GROUP, stride=ROWS_M), :] = columns_of[b][a]
+        ahead = chain(held_map(d, 0), ahead)
+        if d < last:
+            put(d + 1, 0, ahead)
+    start_but(maps_p, 0)
+    put_across(0, ahead)
+
+    def prefix(d):
+        return [send_mr[d, pl.ds(b * comps, comps)] for b in range(comps)]
+
+    behind = held_map(last, 2)
+    across_map = chain(held_map(last, 1), prefix(last))
+    for d in range(last - 1, -1, -1):
+        put(d, 1, across_map)
+        put(d, 2, behind)
+        own = held_map(d, 2)
+        entering = chain(held_map(d, 1), prefix(d)) if d else held_map(0, 1)
+        across_map = join(entering, chain(own, across_map))
+        behind = chain(own, behind)
+    put_across(1, across_map)
+    put_across(2, behind)
     start(maps_2)
+    start_but(maps_q, last)
+    put(0, 0, same)
+    put(last, 1, [0.0 * column for column in same])
+    put(last, 2, same)
     keep_own(send_m2, recv_m2, ROWS_M)
+    recv_mr[spot] = send_mr[spot]
+
+    @pl.when(spot == 0)
+    def _():
+        for i in range(1, GROUP):
+            recv_mr[i, pl.ds(0, 25)] = send_mr[0, pl.ds(0, 25)]
+
+    @pl.when(spot == last)
+    def _():
+        for i in range(last):
+            recv_mr[i, pl.ds(25, 50)] = send_mr[last, pl.ds(25, 50)]
 
     arrive(ends_1)
-    forward_end = recv_v1[0, pl.ds(0, comps)]
-    backward_end = recv_v1[0, pl.ds(comps, comps)]
+
+    def end(d, part):
+        return recv_v1[d, pl.ds(part * comps, comps)]
+
+    reach = [jnp.zeros((comps, quarter, lanes), F32), end(0, 0)]
     for d in range(1, GROUP):
-        turned = recv_v1[d, pl.ds(comps, comps)] + times(held_map(d, 1), forward_end)
-        left = [left_back[d, pl.ds(b * comps, comps)] for b in range(comps)]
-        backward_end = backward_end + times(left, turned)
-        forward_end = recv_v1[d, pl.ds(0, comps)] + times(held_map(d, 0), forward_end)
+        reach.append(end(d, 0) + times(held_map(d, 0), reach[d]))
+    back = [None] * GROUP
+    back[last] = reach[0]
+    back[last - 1] = end(last, 1) + times(held_map(last, 1), reach[last])
+    for d in range(last - 1, 0, -1):
+        back[d - 1] = end(d, 1) + times(held_map(d, 1), reach[d]) + times(held_map(d, 2), back[d])
+    west_out = end(0, 1) + times(held_map(0, 2), back[0])
     for c in range(comps):
-        send_v2[pl.ds(c, GROUP, stride=ROWS_V), :] = forward_end[c]
-        send_v2[pl.ds(8 + c, GROUP, stride=ROWS_V), :] = backward_end[c]
+        send_v2[pl.ds(c, GROUP, stride=ROWS_V), :] = reach[GROUP][c]
+        send_v2[pl.ds(8 + c, GROUP, stride=ROWS_V), :] = west_out[c]
     start(ends_2)
     keep_own(send_v2, recv_v2, ROWS_V)
+    for d in range(GROUP):
+        send_r1[d, pl.ds(0, comps)] = reach[d]
+        send_r1[d, pl.ds(comps, comps)] = back[d]
+    start(back_1)
+    recv_r1[spot] = send_r1[spot]
 
     def apply(start_row, vector):
         return total(
@@ -355,30 +431,26 @@
                 + apply(i * ROWS_M + 50, came)
             )
     start(back_2)
-    keep_own(send_r2, recv_r2, ROWS_V)
-
+    recv_r2[aligned(mine * ROWS_V, ROWS_V), :] = send_r2[aligned(group * ROWS_V, ROWS_V), :]
+
+    arrive_but(maps_p, 0)
+    arrive_but(maps_q, last)
+    arrive(back_1)
     arrive(back_2)
-    came = jnp.stack([recv_r2[pl.ds(c, GROUP, stride=ROWS_V), :] for c in range(comps)])
-    forward_in = []
-    for d in range(GROUP):
-        forward_in.append(came)
-        send_r1[d, pl.ds(0, comps)] = came
-        if d < GROUP - 1:
-            came = recv_v1[d, pl.ds(0, comps)] + times(held_map(d, 0), came)
-    came = jnp.stack([recv_r2[pl.ds(8 + c, GROUP, stride=ROWS_V), :] for c in range(comps)])
-    for d in range(GROUP - 1, -1, -1):
-        send_r1[d, pl.ds(comps, comps)] = came
-        if d > 0:
-            came = (
-                recv_v1[d, pl.ds(comps, comps)] + times(held_map(d, 1), forward_in[d]) + times(held_map(d, 2), came)
-            )
-    start(back_1)
-    recv_r1[spot] = send_r1[spot]
-
-    arrive(back_1)
-    came = [
-        jnp.concatenate([recv_r1[i, c] for i in range(GROUP)], axis=0) for c in range(2 * comps)
-    ]
+    parts = []
+    for i in range(GROUP):
+        into = [
+            jnp.stack([
+                recv_r2[pl.ds(i * quarter * ROWS_V + part * 8 + c, quarter, stride=ROWS_V), :] for c in range(comps)
+            ])
+            for part in range(2)
+        ]
+        block = [[recv_mr[i, pl.ds(part * 25 + b * comps, comps)] for b in range(comps)] for part in range(3)]
+        forward_in = recv_r1[i, pl.ds(0, comps)] + times(block[0], into[0])
+        backward_in = recv_r1[i, pl.ds(comps, comps)] + times(block[1], into[0]) + times(block[2], into[1])
+        parts.append([forward_in[c] for c in range(comps)] + [backward_in[c] for c in range(comps)])
+    came = [jnp.concatenate([part[c] for part in parts], axis=0) for c in range(2 * comps)]
+
     lax.fori_loop(0, planes, forward, came[:comps])
 
     def finish(turn, held):
@@ -391,6 +463,8 @@
     lax.fori_loop(0, planes, finish, came[comps:])
     for copy in halos + maps_a + maps_b + maps_2 + ends_1 + ends_2 + back_2 + back_1:
         copy.wait_send()
+    sent_but(maps_p, 0)
+    sent_but(maps_q, last)
 
 
 def on_device(n, ny, state_field, source, fluid_mask, cell_kind, boundary_side_number, center_matrix,
@@ -425,11 +499,12 @@
             vmem((2, planes * comps, lanes), F32),
             vmem((planes * cells, lanes), F32),
             blocks, blocks, blocks, field, field,
-            maps, maps, ends, ends, ends, ends, vmem((GROUP, 25, quarter, lanes), F32),
-            maps_across, maps_across, ends_across, ends_across, ends_across, ends_across,
+            maps, maps, ends, ends, ends, ends, maps, maps,
+            maps_across, maps_across, ends_across, ends_across, ends_across, vmem((n * ROWS_V, lanes), F32),
             pltpu.SemaphoreType.DMA((11,)),
             pltpu.SemaphoreType.DMA((5,)), pltpu.SemaphoreType.DMA((5,)),
-            pltpu.SemaphoreType.DMA((7, GROUP - 1)), pltpu.SemaphoreType.DMA((7, GROUP - 1)),
+            pltpu.SemaphoreType.DMA((8, GROUP - 1)), pltpu.SemaphoreType.DMA((8, GROUP - 1)),
+            pltpu.SemaphoreType.DMA((n - 1,)), pltpu.SemaphoreType.DMA((n - 1,)),
         ],
         compiler_params=pltpu.CompilerParams(
             collective_id=0, has_side_effects=True, vmem_limit_bytes=61 * 1024 * 1024

time: 38.5 us -> 37.3 us (0.969)
  Pallas kernels: 37.7 us -> 36.2 us
    pallas_call x1, Pallas kernels: 36.6 us -> 35.2 us  [on_device(): pl.pallas_call(functools.partial(kernel, n, ny), out_shape=(pltpu.VMEM(st...]
where the time goes in v5:
time: 37.3 us; the launch traced here: 36.9 us
  Pallas kernels  36.2 us (97%)
  between operations  0.64 us (2%)
    pallas_call x1, Pallas kernels, on_device(): pl.pallas_call(functools.partial(kernel, n, ny), out_shape=(pltpu.VMEM(st...  35.2 us
    pallas_call x1, Pallas kernels, write(): pl.pallas_call(write_kernel, out_shape=(jax.ShapeDtypeStruct(update.shape...  1.07 us

profile of v5, /device:TPU:32, one launch (start us, length us, event | category | flops | bytes accessed | tf_op | source)
XLA Modules:
  0.0 36.9 jit_solution(11854434880465377)
XLA Ops:
  0.6 35.2 %shard_map.122 = (f32[16,5,16,128]{3,2,1,0:T(8,128)S(1)}, f32[1280,128]{1,0:T(8,128)S(1)}) custom-call(f32[16,5,16,128]{3,2,1,0:T(8,128)} %state_hbm.1, f32[16,5,16,128]{3,2,1,0:T(8,128)} %source_hbm.1, s32[256,128]{1,0:T(8,128)} %bitcast.6, s32[256,128]{1,0:T(8,128)} %bitcast.7, s32[256,128]{1,0:T(8,128)} %bitcast.8, f32[16,5,5,16,128]{4,3,2,1,0:T(8,128)} %diag_hbm.1, ...), custom_call_target="tpu_custom_call" | custom-call | tf_op jit(solution)/shard_map/pallas_call | solution.py:486
  35.8 1.1 %shard_map.123 = (f32[16,5,16,128]{3,2,1,0:T(8,128)}, f32[16,5,16,128]{3,2,1,0:T(8,128)}) custom-call(f32[16,5,16,128]{3,2,1,0:T(8,128)S(1)} %get-tuple-element.4.update, f32[16,5,16,128]{3,2,1,0:T(8,128)S(1)} %bitcast.5), custom_call_target="tpu_custom_call" | custom-call | tf_op jit(solution)/shard_map/pallas_call | solution.py:532

commit v6 on v5

--- a/solution.py
+++ b/solution.py
@@ -12,6 +12,7 @@
 GROUP = 4
 MAPS = 75
 ROWS_M = 80
+CHUNKS = 4
 ROWS_V = 16
 
 
@@ -122,8 +123,6 @@
             tf[0, :, b, aligned(half * 8, 8), :] = first[b]
         pack(0, half, lax.fori_loop(1, planes, step, first))
 
-    for half in range(rows // 8):
-        forward_maps(half)
 
     def remote(src, dst, send_sem, recv_sem, where):
         return pltpu.make_async_remote_copy(
@@ -203,6 +202,8 @@
 
     pl.semaphore_wait(barrier, n + 2)
     start(halos)
+    for half in range(rows // 8):
+        forward_maps(half)
     start(maps_a)
 
     def backward_maps(half):
@@ -518,9 +519,11 @@
 
 
 def write_kernel(update, residual, update_out, residual_out, sems):
+    size = update.shape[0] // CHUNKS
     copies = [
-        pltpu.make_async_copy(update, update_out, sems.at[0]),
-        pltpu.make_async_copy(residual, residual_out, sems.at[1]),
+        pltpu.make_async_copy(src.at[pl.ds(i * size, size)], dst.at[pl.ds(i * size, size)], sems.at[k, i])
+        for k, (src, dst) in enumerate(((update, update_out), (residual, residual_out)))
+        for i in range(CHUNKS)
     ]
     for copy in copies:
         copy.start()
@@ -534,7 +537,7 @@
         out_shape=(jax.ShapeDtypeStruct(update.shape, F32), jax.ShapeDtypeStruct(residual.shape, F32)),
         in_specs=[pl.BlockSpec(memory_space=pltpu.VMEM)] * 2,
         out_specs=(pl.BlockSpec(memory_space=pltpu.HBM),) * 2,
-        scratch_shapes=[pltpu.SemaphoreType.DMA((2,))],
+        scratch_shapes=[pltpu.SemaphoreType.DMA((2, CHUNKS))],
         compiler_params=pltpu.CompilerParams(vmem_limit_bytes=1024 * 1024),
     )(update, residual)
 

time: 37.3 us -> 36.9 us (0.989)
  Pallas kernels: 36.2 us -> 35.8 us
    pallas_call x1, Pallas kernels: 35.2 us -> 34.7 us  [on_device(): pl.pallas_call(functools.partial(kernel, n, ny), out_shape=(pltpu.VMEM(st...]
where the time goes in v6:
time: 36.9 us; the launch traced here: 36.5 us
  Pallas kernels  35.8 us (97%)
  between operations  0.64 us (2%)
    pallas_call x1, Pallas kernels, on_device(): pl.pallas_call(functools.partial(kernel, n, ny), out_shape=(pltpu.VMEM(st...  34.7 us
    pallas_call x1, Pallas kernels, write(): pl.pallas_call(write_kernel, out_shape=(jax.ShapeDtypeStruct(update.shape...  1.12 us

profile of v6, /device:TPU:32, one launch (start us, length us, event | category | flops | bytes accessed | tf_op | source)
XLA Modules:
  0.0 36.5 jit_solution(1934331079891738034)
XLA Ops:
  0.6 34.7 %shard_map.122 = (f32[16,5,16,128]{3,2,1,0:T(8,128)S(1)}, f32[1280,128]{1,0:T(8,128)S(1)}) custom-call(f32[16,5,16,128]{3,2,1,0:T(8,128)} %state_hbm.1, f32[16,5,16,128]{3,2,1,0:T(8,128)} %source_hbm.1, s32[256,128]{1,0:T(8,128)} %bitcast.6, s32[256,128]{1,0:T(8,128)} %bitcast.7, s32[256,128]{1,0:T(8,128)} %bitcast.8, f32[16,5,5,16,128]{4,3,2,1,0:T(8,128)} %diag_hbm.1, ...), custom_call_target="tpu_custom_call" | custom-call | tf_op jit(solution)/shard_map/pallas_call | solution.py:487
  35.4 1.1 %shard_map.123 = (f32[16,5,16,128]{3,2,1,0:T(8,128)}, f32[16,5,16,128]{3,2,1,0:T(8,128)}) custom-call(f32[16,5,16,128]{3,2,1,0:T(8,128)S(1)} %get-tuple-element.4.update, f32[16,5,16,128]{3,2,1,0:T(8,128)S(1)} %bitcast.5), custom_call_target="tpu_custom_call" | custom-call | tf_op jit(solution)/shard_map/pallas_call | solution.py:535
